TPU v7x, 32 devices: a whole 2x2x4 slice. The times are simulated.
32 devices in a mesh: grp: 2 (over y), lon: 4 (over z), lat: 2 (over x), ch: 2 (over core).
Axes of the slice: x: 2, y: 2, z: 4, core: 2. Of those that a mesh axis runs over, the one named last changes fastest.
Arguments:
- fields: bfloat16 [69, 512, 512], P(None, ('grp', 'lat'), 'lon'), parts along dimension 1, may hold values from -6 to 6
- land_sea: int32 [256, 512], P('lat', 'lon'), may hold values 0 or 1
- orography: int32 [256, 512], P('lat', 'lon'), may hold values from 0 to 63
- embed_weight: bfloat16 [69, 4, 4, 512], P(None, None, None, 'ch'), may hold values from -0.1875 to 0.1875
- class_table: bfloat16 [128, 512], P(None, 'ch'), may hold values from -5 to 5
- conv_kernel: float32 [2, 7, 7, 512], P(None, None, None, 'ch'), may hold values from -1.75 to 1.75
- conv_bias: float32 [2, 512], P(None, 'ch'), may hold values from -3 to 3
- norm_gain: float32 [2, 512], replicated, may hold values from 0.5 to 1.5
- norm_bias: float32 [2, 512], replicated, may hold values from -3 to 3
- up_proj: bfloat16 [2, 512, 2048], P(None, 'lon', 'ch'), may hold values from -0.25 to 0.25
- up_bias: float32 [2, 2048], replicated, may hold values from -3 to 3
- down_proj: bfloat16 [2, 2048, 512], P(None, 'ch', 'lon'), may hold values from -0.125 to 0.125
- down_bias: float32 [2, 512], replicated, may hold values from -3 to 3
- layer_scale: float32 [2, 512], replicated, may hold values from 0.25 to 1.75
Outputs:
- features: bfloat16 [128, 128, 512], P(('grp', 'lat'), 'lon', 'ch'), parts along dimension 0
There are 2 independent parts, one for each index of `grp`. A program takes and returns all parts, laid end to end along the dimension named above; an argument that names none is the same for every part. Nothing has to cross between parts.
All inputs are finite; a program needn't handle non-finite values. No bound on the sum of `land_sea` on one device may be relied on, other than what follows from the above.
Results may differ from a plain program's by a relative error of at most 0.014.
Values may be sent and summed in bfloat16 or wider, within the bound.
A program may use at most 64 MiB of HBM per device.

v0:
```python
import jax
import jax.numpy as jnp
from jax import lax
from jax.sharding import PartitionSpec as P

PATCH = 4
KERNEL = 7
BLOCKS = 2
HALO = 3


def padded(cells, sides, width, closed):
    for axis, dim in sides:
        count = lax.axis_size(axis)
        ends = count if closed else count - 1
        head = lax.slice_in_dim(cells, 0, width, axis=dim)
        tail = lax.slice_in_dim(cells, cells.shape[dim] - width, cells.shape[dim], axis=dim)
        cells = jnp.concatenate(
            [
                lax.ppermute(tail, axis, [(i, (i + 1) % count) for i in range(ends)]),
                cells,
                lax.ppermute(head, axis, [((i + 1) % count, i) for i in range(ends)]),
            ],
            axis=dim,
        )
    return cells


def embed_tokens(fields, land_sea, orography, embed_weight, class_table):
    var_count, lat_cells, lon_cells = fields.shape
    tok_rows = lat_cells // PATCH
    tok_cols = lon_cells // PATCH
    width = embed_weight.shape[3]
    cell_grid = fields.reshape(var_count, tok_rows, PATCH, tok_cols, PATCH)
    patch_term = jnp.einsum(
        "vrpcq,vpqk->rck", cell_grid, embed_weight, preferred_element_type=jnp.float32
    )
    class_codes = 2 * orography + land_sea
    classes = class_table.shape[0]
    one_hot = (class_codes[..., None] == jnp.arange(classes, dtype=jnp.int32)).astype(jnp.bfloat16)
    class_counts = one_hot.reshape(tok_rows, PATCH, tok_cols, PATCH, classes).sum(axis=(1, 3))
    static_term = jnp.dot(
        class_counts.reshape(tok_rows * tok_cols, classes),
        class_table,
        preferred_element_type=jnp.float32,
    )
    return (
        patch_term + static_term.reshape(tok_rows, tok_cols, width) * (1.0 / (PATCH * PATCH))
    ).astype(jnp.bfloat16)


def depthwise(framed, kernel, bias, tok_rows, tok_cols):
    summed = jnp.zeros((tok_rows, tok_cols, kernel.shape[2]), jnp.float32) + bias
    for row_off in range(KERNEL):
        for col_off in range(KERNEL):
            summed = (
                summed
                + framed[row_off : row_off + tok_rows, col_off : col_off + tok_cols].astype(
                    jnp.float32
                )
                * kernel[row_off, col_off]
            )
    return summed.astype(jnp.bfloat16)


def feed_forward(normed, up_weight, down_weight, bias_up):
    pre = jnp.dot(
        normed,
        lax.all_gather(up_weight, "lon", axis=0, tiled=True),
        preferred_element_type=jnp.float32,
    )
    hidden = jax.nn.gelu(pre + bias_up, approximate=True).astype(jnp.bfloat16)
    return jnp.dot(
        hidden,
        lax.all_gather(down_weight, "lon", axis=1, tiled=True),
        preferred_element_type=jnp.float32,
    )


def body(
    fields,
    land_sea,
    orography,
    embed_weight,
    class_table,
    conv_kernel,
    conv_bias,
    norm_gain,
    norm_bias,
    up_proj,
    up_bias,
    down_proj,
    down_bias,
    layer_scale,
):
    var_count, lat_cells, lon_cells = fields.shape
    tok_rows = lat_cells // PATCH
    tok_cols = lon_cells // PATCH
    channels = norm_gain.shape[1]
    core_index = lax.axis_index("ch")
    token_count = tok_rows * tok_cols
    half_width = embed_weight.shape[3]
    stream = embed_tokens(fields, land_sea, orography, embed_weight, class_table)
    for layer in range(BLOCKS):
        sector_ext = padded(stream, (("lon", 1),), HALO, True)
        framed = padded(sector_ext, (("lat", 0),), HALO, False)
        conv = depthwise(framed, conv_kernel[layer], conv_bias[layer], tok_rows, tok_cols).reshape(
            token_count, half_width
        )
        gain_full = norm_gain[layer]
        shift_full = norm_bias[layer]
        conv_f = conv.astype(jnp.float32)
        row_total, row_square = lax.psum(
            (jnp.sum(conv_f, axis=1), jnp.sum(conv_f * conv_f, axis=1)), "ch"
        )
        average = (row_total / channels)[:, None]
        variance = (row_square / channels)[:, None] - average * average
        gain_share = lax.dynamic_slice_in_dim(gain_full, core_index * half_width, half_width)
        shift_share = lax.dynamic_slice_in_dim(shift_full, core_index * half_width, half_width)
        outgoing = (
            (conv_f - average) * lax.rsqrt(variance + 1e-06) * gain_share + shift_share
        ).astype(jnp.bfloat16)
        arrived = lax.all_to_all(outgoing, "ch", split_axis=0, concat_axis=1, tiled=True)
        up_weight, down_weight = (
            lax.all_gather(up_proj[layer], "ch", axis=1, tiled=True),
            lax.all_gather(down_proj[layer], "ch", axis=0, tiled=True),
        )
        bias_up = up_bias[layer]
        partial_value = feed_forward(arrived, up_weight, down_weight, bias_up)
        update = lax.all_to_all(
            partial_value.astype(jnp.bfloat16), "ch", split_axis=1, concat_axis=0, tiled=True
        ).astype(partial_value.dtype)
        bias_down = lax.dynamic_slice_in_dim(down_bias[layer], core_index * half_width, half_width)
        scale_share = lax.dynamic_slice_in_dim(
            layer_scale[layer], core_index * half_width, half_width
        )
        stream_f = stream.reshape(token_count, half_width).astype(jnp.float32)
        stream = (
            (stream_f + scale_share * (update + bias_down))
            .astype(jnp.bfloat16)
            .reshape(tok_rows, tok_cols, half_width)
        )
    return stream


def solution(mesh):
    in_specs = (
        P(None, ("grp", "lat"), "lon"),
        P("lat", "lon"),
        P("lat", "lon"),
        P(None, None, None, "ch"),
        P(None, "ch"),
        P(None, None, None, "ch"),
        P(None, "ch"),
        P(),
        P(),
        P(None, "lon", "ch"),
        P(),
        P(None, "ch", "lon"),
        P(),
        P(),
    )
    out_specs = P(("grp", "lat"), "lon", "ch")
    return jax.shard_map(body, mesh=mesh, in_specs=in_specs, out_specs=out_specs, check_vma=False)
```

profile of v0, /device:TPU:0, one launch (start us, length us, event | category | flops | bytes accessed | tf_op | source)
XLA Modules:
  0.0 220.5 jit_solution(8120151638113108140)
XLA Ops:
  6.5 1.1 fusion.116
  7.7 2.4 %all-gather = bf16[1,128,2048]{2,1,0:T(8,128)(2,1)} all-gather(bf16[1,128,1024]{2,1,0:T(8,128)(2,1)S(1)} %get-tuple-element.24), channel_id=2, replica_groups=mesh['grp'=2,'lon'=4,'lat'=2,'ch'=2] {'ch'}, dimensions={2}, use_global_device_ids=true | all-gather | bytes 786432 | tf_op jit(solution)/shard_map/all_gather | solution.py:125
  10.2 2.4 %all-gather.2 = bf16[1,2048,128]{2,1,0:T(8,128)(2,1)} all-gather(bf16[1,1024,128]{2,1,0:T(8,128)(2,1)S(1)} %get-tuple-element.28), channel_id=4, replica_groups=mesh['grp'=2,'lon'=4,'lat'=2,'ch'=2] {'ch'}, dimensions={1}, use_global_device_ids=true | all-gather | bytes 786432 | tf_op jit(solution)/shard_map/all_gather | solution.py:126
  12.7 2.3 %all-gather.4 = bf16[1,128,2048]{2,1,0:T(8,128)(2,1)} all-gather(bf16[1,128,1024]{2,1,0:T(8,128)(2,1)S(1)} %get-tuple-element.23), channel_id=6, replica_groups=mesh['grp'=2,'lon'=4,'lat'=2,'ch'=2] {'ch'}, dimensions={2}, use_global_device_ids=true | all-gather | bytes 786432 | tf_op jit(solution)/shard_map/all_gather | solution.py:125
  15.1 4.5 %copy.28 = bf16[69,128,128]{0,2,1:T(8,128)(2,1)} copy(bf16[69,128,128]{2,1,0:T(8,128)(2,1)S(1)} %copy-done.1) | data formatting | bytes 4521984 | tf_op args[0]
  19.6 2.1 eq.16
  21.8 0.8 copy.31
  22.6 2.8 %fusion.17 = bf16[32,32,128]{2,1,0:T(8,128)(2,1)S(1)} fusion(s32[32,4,32,4]{2,3,1,0:T(4,128)S(1)} %copy.31), kind=kLoop, calls=%fused_computation.20 | loop fusion | flops 6160384 | bytes 327680 | tf_op jit(solution)/shard_map/reduce_sum | solution.py:41
  25.5 3.4 %fusion.26 = f32[32,32,256]{2,1,0:T(8,128)S(1)} fusion(bf16[69,32,4,32,4]{0,4,3,2,1:T(4,128)(2,1)} %bitcast.168, bf16[69,4,4,256]{3,2,1,0:T(4,128)(2,1)S(1)} %copy-done.12), kind=kOutput, calls=%fused_computation.29 | convolution fusion | flops 578813952 | bytes 3874816 | tf_op jit(solution)/shard_map/vrpcq,vpqk->rck/dot_general | solution.py:35
  29.0 0.3 fusion.36
  29.4 3.0 %collective-permute-start = (bf16[32,3,256]{2,1,0:T(4,128)(2,1)S(1)}, bf16[32,3,256]{2,1,0:T(4,128)(2,1)S(1)}, u32[]{:S(2)}, u32[]{:S(2)}) collective-permute-start(bf16[32,3,256]{2,1,0:T(4,128)(2,1)S(1)} %get-tuple-element.29), channel_id=1, source_target_pairs={{0,4},{4,8},{8,12},{12,0},{1,5},{5,9},{9,13},{13,1},{2,6},{6,10},{... | collective-permute-start | bytes 147464 | tf_op jit(solution)/shard_map/ppermute | solution.py:20
  32.3 2.1 collective-permute-start.1
  34.4 2.3 %all-gather.6 = bf16[1,2048,128]{2,1,0:T(8,128)(2,1)} all-gather(bf16[1,1024,128]{2,1,0:T(8,128)(2,1)S(1)} %get-tuple-element.27), channel_id=8, replica_groups=mesh['grp'=2,'lon'=4,'lat'=2,'ch'=2] {'ch'}, dimensions={1}, use_global_device_ids=true | all-gather | bytes 786432 | tf_op jit(solution)/shard_map/all_gather | solution.py:126
  37.2 1.5 collective-permute-done
  38.7 2.8 %collective-permute-done.1 = bf16[32,3,256]{2,1,0:T(4,128)(2,1)S(1)} collective-permute-done((bf16[32,3,256]{2,1,0:T(4,128)(2,1)S(1)}, bf16[32,3,256]{2,1,0:T(4,128)(2,1)S(1)}, u32[]{:S(2)}, u32[]{:S(2)}) %collective-permute-start.1) | collective-permute-done | bytes 49184 | tf_op jit(solution)/shard_map/ppermute | solution.py:22
  41.5 3.4 %collective-permute-start.2 = (bf16[3,38,256]{2,1,0:T(8,128)(2,1)S(1)}, bf16[3,38,256]{2,1,0:T(8,128)(2,1)S(1)}, u32[]{:S(2)}, u32[]{:S(2)}) collective-permute-start(bf16[3,38,256]{2,1,0:T(8,128)(2,1)S(1)} %get-tuple-element.21), channel_id=1, source_target_pairs={{0,2},{1,3},{4,6},{5,7},{8,10},{9,11},{12,14},{13,15},{16,18},{17,... | collective-permute-start | bytes 175112 | tf_op jit(solution)/shard_map/ppermute | solution.py:20
  44.9 1.3 collective-permute-start.3
  46.2 0.5 collective-permute-done.2
  46.8 4.3 %collective-permute-done.3 = bf16[3,38,256]{2,1,0:T(8,128)(2,1)S(1)} collective-permute-done((bf16[3,38,256]{2,1,0:T(8,128)(2,1)S(1)}, bf16[3,38,256]{2,1,0:T(8,128)(2,1)S(1)}, u32[]{:S(2)}, u32[]{:S(2)}) %collective-permute-start.3) | collective-permute-done | bytes 58400 | tf_op jit(solution)/shard_map/ppermute | solution.py:22
  51.0 0.4 maximum_maximum_fusion
  51.5 8.7 %convert_reduce_fusion.1 = (f32[32,32]{1,0:T(8,128)S(1)}, f32[32,32]{1,0:T(8,128)S(1)}, bf16[32,32,256]{2,1,0:T(8,128)(2,1)S(1)}) fusion(f32[256]{0:T(256)S(1)} %bitcast.243, bf16[35,38,256]{2,1,0:T(8,128)(2,1)S(1)} %get-tuple-element.20, f32[256]{0:T(256)S(1)} %bitcast.244, f32[256]{0:T(256)S(1)} %bitcast.245, f32[256]{0:T(256)S(1)} %bitcast.246, ...), kind=kLoop, calls=%fused_computation.132 | loop fusion | flops 44562432 | bytes 23226368 | tf_op jit(solution)/shard_map/reduce_sum | solution.py:114
  60.3 2.5 %all-reduce.1 = (f32[1024]{0:T(1024)S(1)}, f32[1024]{0:T(1024)S(1)}) all-reduce(f32[1024]{0:T(1024)S(1)} %reduce_sum.60, f32[1024]{0:T(1024)S(1)} %reduce_sum.58), channel_id=1, replica_groups=mesh['grp'=2,'lon'=4,'lat'=2,'ch'=2] {'ch'}, use_global_device_ids=true, to_apply=%region_4.0 | all-reduce | flops 2048 | bytes 16384 | tf_op jit(solution)/shard_map/psum | solution.py:113
  62.8 0.2 copy.33
  63.0 0.2 add_convert_fusion.1
  63.2 4.2 %all_to_all.58 = bf16[2,512,256]{1,2,0:T(8,128)(2,1)S(1)} all-to-all(bf16[2,512,256]{1,2,0:T(8,128)(2,1)S(1)} %add_convert_fusion.1), channel_id=1, replica_groups=mesh['grp'=2,'lon'=4,'lat'=2,'ch'=2] {'ch'}, dimensions={0} | all-to-all | bytes 1048576 | tf_op jit(solution)/shard_map/all_to_all | solution.py:123
  67.4 40.8 %all-gather.15.cloned.1.call-done = bf16[1,2048,512]{2,1,0:T(8,128)(2,1)} async-done(((bf16[1,2048,128]{2,1,0:T(8,128)(2,1)}), bf16[1,2048,512]{2,1,0:T(8,128)(2,1)}) %all-gather.15.cloned.1.call-update) | async-done | bytes 2097168 | tf_op jit(solution)/shard_map/all_gather | solution.py:75
  108.1 5.3 %fusion.30 = bf16[512,512]{0,1:T(8,128)(2,1)S(1)} fusion(bf16[1,2048,512]{2,1,0:T(8,128)(2,1)} %all-gather.15.cloned.1.call-done, bf16[512,512]{0,1:T(8,128)(2,1)S(1)} %bitcast.172, bf16[1,512,2048]{2,1,0:T(8,128)(2,1)} %all-gather.13.cloned.1.call-done, f32[2048]{0:T(1024)S(1)} %bitcast.176), kind=kOutput, calls=%fused_computation.36 | convolution fusion | flops 2158231552 | bytes 5251072 | tf_op jit(solution)/shard_map/dot_general | solution.py:73
  113.5 0.2 copy.34
  113.7 4.2 %all_to_all.59 = bf16[512,2,256]{2,0,1:T(8,128)(2,1)S(1)} all-to-all(bf16[512,2,256]{2,0,1:T(8,128)(2,1)S(1)} %copy.34), channel_id=1, replica_groups=mesh['grp'=2,'lon'=4,'lat'=2,'ch'=2] {'ch'}, dimensions={1} | all-to-all | bytes 1048576 | tf_op jit(solution)/shard_map/all_to_all | solution.py:130
  118.2 0.2 collective-permute-start.4
  118.4 3.6 %collective-permute-start.5 = (bf16[32,3,256]{2,1,0:T(4,128)(2,1)S(1)}, bf16[32,3,256]{2,1,0:T(4,128)(2,1)S(1)}, u32[]{:S(2)}, u32[]{:S(2)}) collective-permute-start(bf16[32,3,256]{2,1,0:T(4,128)(2,1)S(1)} %get-tuple-element.26), channel_id=1, source_target_pairs={{4,0},{8,4},{12,8},{0,12},{5,1},{9,5},{13,9},{1,13},{6,2},{10,6},{... | collective-permute-start | bytes 147464 | tf_op jit(solution)/shard_map/ppermute | solution.py:22
  122.1 4.3 %collective-permute-done.4 = bf16[32,3,256]{2,1,0:T(4,128)(2,1)S(1)} collective-permute-done((bf16[32,3,256]{2,1,0:T(4,128)(2,1)S(1)}, bf16[32,3,256]{2,1,0:T(4,128)(2,1)S(1)}, u32[]{:S(2)}, u32[]{:S(2)}) %collective-permute-start.4) | collective-permute-done | bytes 49184 | tf_op jit(solution)/shard_map/ppermute | solution.py:20
  126.3 0.7 collective-permute-done.5
  127.1 3.4 %collective-permute-start.6 = (bf16[3,38,256]{2,1,0:T(8,128)(2,1)S(1)}, bf16[3,38,256]{2,1,0:T(8,128)(2,1)S(1)}, u32[]{:S(2)}, u32[]{:S(2)}) collective-permute-start(bf16[3,38,256]{2,1,0:T(8,128)(2,1)S(1)} %get-tuple-element.17), channel_id=1, source_target_pairs={{0,2},{1,3},{4,6},{5,7},{8,10},{9,11},{12,14},{13,15},{16,18},{17,... | collective-permute-start | bytes 175112 | tf_op jit(solution)/shard_map/ppermute | solution.py:20
  130.4 1.3 collective-permute-start.7
  131.7 0.5 collective-permute-done.6
  132.3 4.3 %collective-permute-done.7 = bf16[3,38,256]{2,1,0:T(8,128)(2,1)S(1)} collective-permute-done((bf16[3,38,256]{2,1,0:T(8,128)(2,1)S(1)}, bf16[3,38,256]{2,1,0:T(8,128)(2,1)S(1)}, u32[]{:S(2)}, u32[]{:S(2)}) %collective-permute-start.7) | collective-permute-done | bytes 58400 | tf_op jit(solution)/shard_map/ppermute | solution.py:22
  136.5 0.4 maximum_maximum_fusion.1
  137.0 8.7 %convert_reduce_fusion = (f32[32,32]{1,0:T(8,128)S(1)}, f32[32,32]{1,0:T(8,128)S(1)}, bf16[32,32,256]{2,1,0:T(8,128)(2,1)S(1)}) fusion(f32[256]{0:T(256)S(1)} %bitcast.205, bf16[35,38,256]{2,1,0:T(8,128)(2,1)S(1)} %get-tuple-element.16, f32[256]{0:T(256)S(1)} %bitcast.206, f32[256]{0:T(256)S(1)} %bitcast.207, f32[256]{0:T(256)S(1)} %bitcast.208, ...), kind=kLoop, calls=%fused_computation.131 | loop fusion | flops 44562432 | bytes 23226368 | tf_op jit(solution)/shard_map/reduce_sum | solution.py:114
  145.8 2.5 %all-reduce = (f32[1024]{0:T(1024)S(1)}, f32[1024]{0:T(1024)S(1)}) all-reduce(f32[1024]{0:T(1024)S(1)} %reduce_sum.64, f32[1024]{0:T(1024)S(1)} %reduce_sum.62), channel_id=1, replica_groups=mesh['grp'=2,'lon'=4,'lat'=2,'ch'=2] {'ch'}, use_global_device_ids=true, to_apply=%region_8.0 | all-reduce | flops 2048 | bytes 16384 | tf_op jit(solution)/shard_map/psum | solution.py:113
  148.2 0.2 copy.36
  148.5 1.0 add_convert_fusion
  149.5 3.5 %all-to-all-start.2 = ((bf16[2,512,256]{1,2,0:T(8,128)(2,1)}), bf16[2,512,256]{1,2,0:T(8,128)(2,1)S(1)}, u32[]{:S(2)}, u32[]{:S(2)}) async-start(bf16[2,512,256]{1,2,0:T(8,128)(2,1)} %add_convert_fusion), calls=%async_computation.2 | async-start | bytes 1048576 | tf_op jit(solution)/shard_map/all_to_all | solution.py:123
  153.0 3.7 %all-gather.17.cloned.1.call-done = bf16[1,512,2048]{2,1,0:T(8,128)(2,1)} async-done(((bf16[1,128,2048]{2,1,0:T(8,128)(2,1)}), bf16[1,512,2048]{2,1,0:T(8,128)(2,1)}) %all-gather.17.cloned.1.call-update) | async-done | bytes 2097168 | tf_op jit(solution)/shard_map/all_gather | solution.py:69
  156.7 46.4 %all-gather.19.cloned.1.call-done = bf16[1,2048,512]{2,1,0:T(8,128)(2,1)} async-done(((bf16[1,2048,128]{2,1,0:T(8,128)(2,1)}), bf16[1,2048,512]{2,1,0:T(8,128)(2,1)}) %all-gather.19.cloned.1.call-update) | async-done | bytes 2097168 | tf_op jit(solution)/shard_map/all_gather | solution.py:75
  203.2 5.3 %fusion.33 = bf16[512,512]{0,1:T(8,128)(2,1)S(1)} fusion(bf16[1,2048,512]{2,1,0:T(8,128)(2,1)} %all-gather.19.cloned.1.call-done, bf16[512,512]{0,1:T(8,128)(2,1)S(1)} %bitcast.171, bf16[1,512,2048]{2,1,0:T(8,128)(2,1)} %all-gather.17.cloned.1.call-done, f32[2048]{0:T(1024)S(1)} %bitcast.175), kind=kOutput, calls=%fused_computation.37 | convolution fusion | flops 2158231552 | bytes 5251072 | tf_op jit(solution)/shard_map/dot_general | solution.py:73
  208.7 4.2 %all_to_all.60 = bf16[512,2,256]{2,0,1:T(8,128)(2,1)S(1)} all-to-all(bf16[512,2,256]{2,0,1:T(8,128)(2,1)S(1)} %copy.37), channel_id=1, replica_groups=mesh['grp'=2,'lon'=4,'lat'=2,'ch'=2] {'ch'}, dimensions={1} | all-to-all | bytes 1048576 | tf_op jit(solution)/shard_map/all_to_all | solution.py:130
  213.0 1.0 fusion.92
  (74 shorter events, 1.7 us)
Async XLA Ops:
  6.5 22.4 %copy-start = (bf16[128,256]{1,0:T(8,128)(2,1)S(1)}, bf16[128,256]{1,0:T(8,128)(2,1)}, u32[]{:S(2)}) copy-start(bf16[128,256]{1,0:T(8,128)(2,1)} %param.18) | copy-start | bytes 196612
  6.5 3.6 %copy-start.2 = (bf16[2,1024,128]{2,1,0:T(8,128)(2,1)S(1)}, bf16[2,1024,128]{2,1,0:T(8,128)(2,1)}, u32[]{:S(2)}) copy-start(bf16[2,1024,128]{2,1,0:T(8,128)(2,1)} %param.25) | copy-start | bytes 1572868
  6.5 60.8 %all-gather.13.cloned.1.call-start = ((), (), s32[]{:S(2)}) async-start(), calls=%async_computation.4 | async-start | bytes 2621440 | tf_op jit(solution)/shard_map/all_gather | solution.py:69
  10.1 5.1 %copy-start.1 = (bf16[69,128,128]{2,1,0:T(8,128)(2,1)S(1)}, bf16[69,128,128]{2,1,0:T(8,128)(2,1)}, u32[]{:S(2)}) copy-start(bf16[69,128,128]{2,1,0:T(8,128)(2,1)} %param.14) | copy-start | bytes 6782980
  10.1 98.0 %all-gather.15.cloned.1.call-start = ((), (), s32[]{:S(2)}) async-start(), calls=%async_computation.5 | async-start | bytes 2621440 | tf_op jit(solution)/shard_map/all_gather | solution.py:75
  12.7 144.1 %all-gather.17.cloned.1.call-start = ((), (), s32[]{:S(2)}) async-start(), calls=%async_computation.6 | async-start | bytes 2621440 | tf_op jit(solution)/shard_map/all_gather | solution.py:69
  15.1 4.6 %copy-start.4 = (s32[128,128]{1,0:T(8,128)S(1)}, s32[128,128]{1,0:T(8,128)}, u32[]{:S(2)}) copy-start(s32[128,128]{1,0:T(8,128)} %param.15) | copy-start | bytes 196612
  15.1 4.5 %copy-start.5 = (s32[128,128]{1,0:T(8,128)S(1)}, s32[128,128]{1,0:T(8,128)}, u32[]{:S(2)}) copy-start(s32[128,128]{1,0:T(8,128)} %param.16) | copy-start | bytes 196612
  15.1 188.1 %all-gather.19.cloned.1.call-start = ((), (), s32[]{:S(2)}) async-start(), calls=%async_computation.7 | async-start | bytes 2621440 | tf_op jit(solution)/shard_map/all_gather | solution.py:75
  19.6 5.9 %copy-start.12 = (bf16[69,4,4,256]{3,2,1,0:T(4,128)(2,1)S(1)}, bf16[69,4,4,256]{3,2,1,0:T(4,128)(2,1)}, u32[]{:S(2)}) copy-start(bf16[69,4,4,256]{3,2,1,0:T(4,128)(2,1)} %param.17) | copy-start | bytes 1695748
  28.9 7.8 %copy-start.3 = (f32[2,7,7,256]{3,0,2,1:T(2,128)S(1)}, f32[2,7,7,256]{3,0,2,1:T(2,128)}, u32[]{:S(2)}) copy-start(f32[2,7,7,256]{3,0,2,1:T(2,128)} %param.19) | copy-start | bytes 301060
  28.9 8.1 %copy-start.11 = (f32[2,256]{1,0:T(2,128)S(1)}, f32[2,256]{1,0:T(2,128)}, u32[]{:S(2)}) copy-start(f32[2,256]{1,0:T(2,128)} %param.20) | copy-start | bytes 6148
  29.0 8.1 %copy-start.7 = (f32[2,512]{1,0:T(2,128)S(1)}, f32[2,512]{1,0:T(2,128)}, u32[]{:S(2)}) copy-start(f32[2,512]{1,0:T(2,128)} %param.21) | copy-start | bytes 12292
  29.0 8.1 %copy-start.8 = (f32[2,512]{1,0:T(2,128)S(1)}, f32[2,512]{1,0:T(2,128)}, u32[]{:S(2)}) copy-start(f32[2,512]{1,0:T(2,128)} %param.22) | copy-start | bytes 12292
  29.0 8.1 %copy-start.6 = (f32[2,2048]{1,0:T(2,128)S(1)}, f32[2,2048]{1,0:T(2,128)}, u32[]{:S(2)}) copy-start(f32[2,2048]{1,0:T(2,128)} %param.24) | copy-start | bytes 49156
  29.0 8.1 %copy-start.9 = (f32[2,512]{1,0:T(2,128)S(1)}, f32[2,512]{1,0:T(2,128)}, u32[]{:S(2)}) copy-start(f32[2,512]{1,0:T(2,128)} %param.27) | copy-start | bytes 12292
  29.0 8.1 %copy-start.10 = (f32[2,512]{1,0:T(2,128)S(1)}, f32[2,512]{1,0:T(2,128)}, u32[]{:S(2)}) copy-start(f32[2,512]{1,0:T(2,128)} %param.26) | copy-start | bytes 12292
  29.4 9.3 %collective-permute-start = (bf16[32,3,256]{2,1,0:T(4,128)(2,1)S(1)}, bf16[32,3,256]{2,1,0:T(4,128)(2,1)S(1)}, u32[]{:S(2)}, u32[]{:S(2)}) collective-permute-start(bf16[32,3,256]{2,1,0:T(4,128)(2,1)S(1)} %get-tuple-element.29), channel_id=1, source_target_pairs={{0,4},{4,8},{8,12},{12,0},{1,5},{5,9},{9,13},{13,1},{2,6},{6,10},{... | collective-permute-start | bytes 147464 | tf_op jit(solution)/shard_map/ppermute | solution.py:20
  32.3 9.1 %collective-permute-start.1 = (bf16[32,3,256]{2,1,0:T(4,128)(2,1)S(1)}, bf16[32,3,256]{2,1,0:T(4,128)(2,1)S(1)}, u32[]{:S(2)}, u32[]{:S(2)}) collective-permute-start(bf16[32,3,256]{2,1,0:T(4,128)(2,1)S(1)} %get-tuple-element.30), channel_id=1, source_target_pairs={{4,0},{8,4},{12,8},{0,12},{5,1},{9,5},{13,9},{1,13},{6,2},{10,6},{... | collective-permute-start | bytes 147464 | tf_op jit(solution)/shard_map/ppermute | solution.py:22
  41.5 5.3 %collective-permute-start.2 = (bf16[3,38,256]{2,1,0:T(8,128)(2,1)S(1)}, bf16[3,38,256]{2,1,0:T(8,128)(2,1)S(1)}, u32[]{:S(2)}, u32[]{:S(2)}) collective-permute-start(bf16[3,38,256]{2,1,0:T(8,128)(2,1)S(1)} %get-tuple-element.21), channel_id=1, source_target_pairs={{0,2},{1,3},{4,6},{5,7},{8,10},{9,11},{12,14},{13,15},{16,18},{17,... | collective-permute-start | bytes 175112 | tf_op jit(solution)/shard_map/ppermute | solution.py:20
  44.9 6.1 %collective-permute-start.3 = (bf16[3,38,256]{2,1,0:T(8,128)(2,1)S(1)}, bf16[3,38,256]{2,1,0:T(8,128)(2,1)S(1)}, u32[]{:S(2)}, u32[]{:S(2)}) collective-permute-start(bf16[3,38,256]{2,1,0:T(8,128)(2,1)S(1)} %get-tuple-element.22), channel_id=1, source_target_pairs={{2,0},{3,1},{6,4},{7,5},{10,8},{11,9},{14,12},{15,13},{18,16},{19,... | collective-permute-start | bytes 175112 | tf_op jit(solution)/shard_map/ppermute | solution.py:22
  118.2 8.2 %collective-permute-start.4 = (bf16[32,3,256]{2,1,0:T(4,128)(2,1)S(1)}, bf16[32,3,256]{2,1,0:T(4,128)(2,1)S(1)}, u32[]{:S(2)}, u32[]{:S(2)}) collective-permute-start(bf16[32,3,256]{2,1,0:T(4,128)(2,1)S(1)} %get-tuple-element.25), channel_id=1, source_target_pairs={{0,4},{4,8},{8,12},{12,0},{1,5},{5,9},{9,13},{13,1},{2,6},{6,10},{... | collective-permute-start | bytes 147464 | tf_op jit(solution)/shard_map/ppermute | solution.py:20
  118.4 8.6 %collective-permute-start.5 = (bf16[32,3,256]{2,1,0:T(4,128)(2,1)S(1)}, bf16[32,3,256]{2,1,0:T(4,128)(2,1)S(1)}, u32[]{:S(2)}, u32[]{:S(2)}) collective-permute-start(bf16[32,3,256]{2,1,0:T(4,128)(2,1)S(1)} %get-tuple-element.26), channel_id=1, source_target_pairs={{4,0},{8,4},{12,8},{0,12},{5,1},{9,5},{13,9},{1,13},{6,2},{10,6},{... | collective-permute-start | bytes 147464 | tf_op jit(solution)/shard_map/ppermute | solution.py:22
  127.1 5.2 %collective-permute-start.6 = (bf16[3,38,256]{2,1,0:T(8,128)(2,1)S(1)}, bf16[3,38,256]{2,1,0:T(8,128)(2,1)S(1)}, u32[]{:S(2)}, u32[]{:S(2)}) collective-permute-start(bf16[3,38,256]{2,1,0:T(8,128)(2,1)S(1)} %get-tuple-element.17), channel_id=1, source_target_pairs={{0,2},{1,3},{4,6},{5,7},{8,10},{9,11},{12,14},{13,15},{16,18},{17,... | collective-permute-start | bytes 175112 | tf_op jit(solution)/shard_map/ppermute | solution.py:20
  130.4 6.1 %collective-permute-start.7 = (bf16[3,38,256]{2,1,0:T(8,128)(2,1)S(1)}, bf16[3,38,256]{2,1,0:T(8,128)(2,1)S(1)}, u32[]{:S(2)}, u32[]{:S(2)}) collective-permute-start(bf16[3,38,256]{2,1,0:T(8,128)(2,1)S(1)} %get-tuple-element.18), channel_id=1, source_target_pairs={{2,0},{3,1},{6,4},{7,5},{10,8},{11,9},{14,12},{15,13},{18,16},{19,... | collective-permute-start | bytes 175112 | tf_op jit(solution)/shard_map/ppermute | solution.py:22
  149.5 53.7 %all-to-all-start.2 = ((bf16[2,512,256]{1,2,0:T(8,128)(2,1)}), bf16[2,512,256]{1,2,0:T(8,128)(2,1)S(1)}, u32[]{:S(2)}, u32[]{:S(2)}) async-start(bf16[2,512,256]{1,2,0:T(8,128)(2,1)} %add_convert_fusion), calls=%async_computation.2 | async-start | bytes 1048576 | tf_op jit(solution)/shard_map/all_to_all | solution.py:123
Sparse Core Ops, SparseCore 0:
  10.2 51.3 all-gather.12
  63.1 44.9 all-gather.14
  109.7 46.9 all-gather.16
  158.1 44.9 all-gather.18
where the time goes:
time: 221 us; the launch traced here: 220 us
  waiting for transfers between devices  110 us (50%)
  blocking collectives  26.8 us (12%)
  other arithmetic  23.7 us (11%)
  starting transfers between devices  21.9 us (10%)
  matrix products  14.4 us (7%)
  between operations  13.6 us (6%)
  local copies, waits for them, and re-layouts  10.2 us (5%)
    all_gather x2, waiting for transfers between devices, feed_forward(): lax.all_gather(down_weight, 'lon', axis=1, tiled=True)  87.2 us
    reduce_sum x2, other arithmetic, body(): jnp.sum(conv_f, axis=1)  17.3 us
    ppermute x4, waiting for transfers between devices, padded(): lax.ppermute(head, axis, [((i + 1) % count, i) for i in range(ends)])  12 us
    dot_general x2, matrix products, feed_forward(): jnp.dot(hidden, lax.all_gather(down_weight, 'lon', axis=1, tiled=True), p...  10.7 us
    ppermute x4, starting transfers between devices, padded(): lax.ppermute(tail, axis, [(i, (i + 1) % count) for i in range(ends)])  10 us
    all_to_all x2, blocking collectives, body(): lax.all_to_all(partial_value.astype(jnp.bfloat16), 'ch', split_axis=1, co...  8.31 us
    ppermute x4, starting transfers between devices, padded(): lax.ppermute(head, axis, [((i + 1) % count, i) for i in range(ends)])  8.3 us
    ppermute x4, waiting for transfers between devices, padded(): lax.ppermute(tail, axis, [(i, (i + 1) % count) for i in range(ends)])  6.82 us
  transfers between devices with their start and end apart: 13, of which 11 were waited for; matrix products, arithmetic and copies ran while one was open for 18% of the time, Pallas kernels for 0%

commit v1 on v0

--- a/solution.py
+++ b/solution.py
@@ -63,18 +63,11 @@
     return summed.astype(jnp.bfloat16)
 
 
-def feed_forward(normed, up_weight, down_weight, bias_up):
-    pre = jnp.dot(
-        normed,
-        lax.all_gather(up_weight, "lon", axis=0, tiled=True),
-        preferred_element_type=jnp.float32,
-    )
-    hidden = jax.nn.gelu(pre + bias_up, approximate=True).astype(jnp.bfloat16)
-    return jnp.dot(
-        hidden,
-        lax.all_gather(down_weight, "lon", axis=1, tiled=True),
-        preferred_element_type=jnp.float32,
-    )
+def gather_rows(weight, spare):
+    count = lax.axis_size(spare)
+    rows = weight.shape[0] // count
+    share = lax.dynamic_slice_in_dim(weight, lax.axis_index(spare) * rows, rows)
+    return lax.all_gather(share, ("lon", spare), axis=0, tiled=True)
 
 
 def body(
@@ -100,6 +93,13 @@
     core_index = lax.axis_index("ch")
     token_count = tok_rows * tok_cols
     half_width = embed_weight.shape[3]
+    hid = up_proj.shape[2]
+    sectors = lax.axis_size("lon")
+    weights = []
+    for layer in range(BLOCKS):
+        up = gather_rows(up_proj[layer], "lat")
+        down = gather_rows(down_proj[layer], "grp").reshape(sectors, hid, channels // sectors)
+        weights.append((up, down))
     stream = embed_tokens(fields, land_sea, orography, embed_weight, class_table)
     for layer in range(BLOCKS):
         sector_ext = padded(stream, (("lon", 1),), HALO, True)
@@ -107,29 +107,24 @@
         conv = depthwise(framed, conv_kernel[layer], conv_bias[layer], tok_rows, tok_cols).reshape(
             token_count, half_width
         )
-        gain_full = norm_gain[layer]
-        shift_full = norm_bias[layer]
-        conv_f = conv.astype(jnp.float32)
-        row_total, row_square = lax.psum(
-            (jnp.sum(conv_f, axis=1), jnp.sum(conv_f * conv_f, axis=1)), "ch"
-        )
-        average = (row_total / channels)[:, None]
-        variance = (row_square / channels)[:, None] - average * average
-        gain_share = lax.dynamic_slice_in_dim(gain_full, core_index * half_width, half_width)
-        shift_share = lax.dynamic_slice_in_dim(shift_full, core_index * half_width, half_width)
-        outgoing = (
-            (conv_f - average) * lax.rsqrt(variance + 1e-06) * gain_share + shift_share
+        conv_f = lax.all_gather(conv, "ch", axis=1, tiled=True).astype(jnp.float32)
+        average = jnp.sum(conv_f, axis=1, keepdims=True) / channels
+        variance = jnp.sum(conv_f * conv_f, axis=1, keepdims=True) / channels - average * average
+        normed = (
+            (conv_f - average) * lax.rsqrt(variance + 1e-06) * norm_gain[layer] + norm_bias[layer]
         ).astype(jnp.bfloat16)
-        arrived = lax.all_to_all(outgoing, "ch", split_axis=0, concat_axis=1, tiled=True)
-        up_weight, down_weight = (
-            lax.all_gather(up_proj[layer], "ch", axis=1, tiled=True),
-            lax.all_gather(down_proj[layer], "ch", axis=0, tiled=True),
-        )
-        bias_up = up_bias[layer]
-        partial_value = feed_forward(arrived, up_weight, down_weight, bias_up)
-        update = lax.all_to_all(
-            partial_value.astype(jnp.bfloat16), "ch", split_axis=1, concat_axis=0, tiled=True
-        ).astype(partial_value.dtype)
+        up, down = weights[layer]
+        bias_up = lax.dynamic_slice_in_dim(up_bias[layer], core_index * hid, hid)
+        pre = jnp.dot(normed, up, preferred_element_type=jnp.float32)
+        hidden = jax.nn.gelu(pre + bias_up, approximate=True).astype(jnp.bfloat16)
+        partial_sum = jnp.einsum(
+            "th,zhk->tzk", hidden, down, preferred_element_type=jnp.float32
+        ).reshape(token_count, channels)
+        mine = lax.dynamic_slice_in_dim(partial_sum, core_index * half_width, half_width, axis=1)
+        other = lax.dynamic_slice_in_dim(
+            partial_sum, (1 - core_index) * half_width, half_width, axis=1
+        ).astype(jnp.bfloat16)
+        update = mine + lax.ppermute(other, "ch", [(0, 1), (1, 0)]).astype(jnp.float32)
         bias_down = lax.dynamic_slice_in_dim(down_bias[layer], core_index * half_width, half_width)
         scale_share = lax.dynamic_slice_in_dim(
             layer_scale[layer], core_index * half_width, half_width

time: 221 us -> 253 us (1.14)
  waiting for transfers between devices: 110 us -> 165 us
  blocking collectives: 26.8 us -> 0 us
  local copies, waits for them, and re-layouts: 10.2 us -> 17.7 us
  starting transfers between devices: 21.9 us -> 17.2 us
    all_gather x4 -> x6, waiting for transfers between devices: 91 us -> 145 us  [the longest x4 132 us: gather_rows(): return lax.all_gather(share, ('lon', spare), axis=0, tiled=True)]
    convert_element_type x4 -> x2, other arithmetic: 1.4 us -> 17.6 us  [depthwise(): return summed.astype(jnp.bfloat16)]
    reduce_sum x2, other arithmetic: 17.3 us -> 3.18 us  [body(): average = jnp.sum(conv_f, axis=1, keepdims=True) / channels]
    all_to_all x3 -> x0, blocking collectives: 12.5 us -> none  [the longest x2 8.31 us: body(): lax.all_to_all(partial_value.astype(jnp.bfloat16), 'ch', split_axis=1, co...]
    all_gather x4 -> x0, blocking collectives: 9.46 us -> none  [the longest x2 4.75 us: body(): lax.all_gather(down_proj[layer], 'ch', axis=0, tiled=True)]
    psum x2 -> x0, blocking collectives: 4.92 us -> none  [body(): lax.psum((jnp.sum(conv_f, axis=1), jnp.sum(conv_f * conv_f, axis=1)), 'ch')]
    dot_general x0 -> x2, local copies, waits for them, and re-layouts: none -> 4.54 us  [body(): jnp.einsum('th,zhk->tzk', hidden, down, preferred_element_type=jnp.float32)]
    ppermute x0 -> x2, waiting for transfers between devices: none -> 3.7 us  [body(): lax.ppermute(other, 'ch', [(0, 1), (1, 0)]).astype(jnp.float32)]
  transfers between devices with their start and end apart: 13 -> 16, of which waited for: 11 -> 16; matrix products, arithmetic and copies ran while one was open for 18% -> 10% of each run, Pallas kernels for 0% -> 0%
where the time goes in v1:
time: 253 us; the launch traced here: 252 us
  waiting for transfers between devices  165 us (65%)
  other arithmetic  25.8 us (10%)
  local copies, waits for them, and re-layouts  17.7 us (7%)
  starting transfers between devices  17.2 us (7%)
  between operations  13.9 us (5%)
  matrix products  12.8 us (5%)
    all_gather x4, waiting for transfers between devices, gather_rows(): return lax.all_gather(share, ('lon', spare), axis=0, tiled=True)  132 us
    convert_element_type x2, other arithmetic, depthwise(): return summed.astype(jnp.bfloat16)  17.6 us
    all_gather x2, waiting for transfers between devices, body(): conv_f = lax.all_gather(conv, 'ch', axis=1, tiled=True).astype(jnp.float32)  12.9 us
    ppermute x4, waiting for transfers between devices, padded(): lax.ppermute(head, axis, [((i + 1) % count, i) for i in range(ends)])  9.75 us
    dot_general x2, matrix products, body(): jnp.einsum('th,zhk->tzk', hidden, down, preferred_element_type=jnp.float32)  9.07 us
    ppermute x4, starting transfers between devices, padded(): lax.ppermute(tail, axis, [(i, (i + 1) % count) for i in range(ends)])  8.85 us
    ppermute x4, starting transfers between devices, padded(): lax.ppermute(head, axis, [((i + 1) % count, i) for i in range(ends)])  7.97 us
    ppermute x4, waiting for transfers between devices, padded(): lax.ppermute(tail, axis, [(i, (i + 1) % count) for i in range(ends)])  6.27 us
  transfers between devices with their start and end apart: 16, of which 16 were waited for; matrix products, arithmetic and copies ran while one was open for 10% of the time, Pallas kernels for 0%

profile of v1, /device:TPU:0, one launch (start us, length us, event | category | flops | bytes accessed | tf_op | source)
XLA Modules:
  0.0 252.3 jit_solution(17217256743001616833)
XLA Ops:
  6.5 6.1 %copy.29 = bf16[69,128,128]{0,2,1:T(8,128)(2,1)} copy(bf16[69,128,128]{2,1,0:T(8,128)(2,1)} %param.14) | data formatting | bytes 4521984 | tf_op args[0]
  12.6 2.1 eq.16
  14.8 0.8 copy.32
  15.6 2.8 %fusion.17 = bf16[32,32,128]{2,1,0:T(8,128)(2,1)S(1)} fusion(s32[32,4,32,4]{2,3,1,0:T(4,128)S(1)} %copy.32), kind=kLoop, calls=%fused_computation.20 | loop fusion | flops 6160384 | bytes 327680 | tf_op jit(solution)/shard_map/reduce_sum | solution.py:41
  18.5 3.4 %fusion.30 = f32[32,32,256]{2,1,0:T(8,128)S(1)} fusion(bf16[69,32,4,32,4]{0,4,3,2,1:T(4,128)(2,1)} %bitcast.156, bf16[69,4,4,256]{3,2,1,0:T(4,128)(2,1)S(1)} %copy-done.13), kind=kOutput, calls=%fused_computation.39 | convolution fusion | flops 578813952 | bytes 3874816 | tf_op jit(solution)/shard_map/vrpcq,vpqk->rck/dot_general | solution.py:35
  21.9 0.3 fusion.34
  22.3 3.1 %collective-permute-start = (bf16[32,3,256]{2,1,0:T(4,128)(2,1)S(1)}, bf16[32,3,256]{2,1,0:T(4,128)(2,1)S(1)}, u32[]{:S(2)}, u32[]{:S(2)}) collective-permute-start(bf16[32,3,256]{2,1,0:T(4,128)(2,1)S(1)} %get-tuple-element.21), channel_id=1, source_target_pairs={{0,4},{4,8},{8,12},{12,0},{1,5},{5,9},{9,13},{13,1},{2,6},{6,10},{... | collective-permute-start | bytes 147464 | tf_op jit(solution)/shard_map/ppermute | solution.py:20
  25.4 2.1 collective-permute-start.1
  27.6 2.1 collective-permute-done
  29.8 0.5 collective-permute-done.1
  30.4 3.4 %collective-permute-start.2 = (bf16[3,38,256]{2,1,0:T(8,128)(2,1)S(1)}, bf16[3,38,256]{2,1,0:T(8,128)(2,1)S(1)}, u32[]{:S(2)}, u32[]{:S(2)}) collective-permute-start(bf16[3,38,256]{2,1,0:T(8,128)(2,1)S(1)} %get-tuple-element.15), channel_id=1, source_target_pairs={{0,2},{1,3},{4,6},{5,7},{8,10},{9,11},{12,14},{13,15},{16,18},{17,... | collective-permute-start | bytes 175112 | tf_op jit(solution)/shard_map/ppermute | solution.py:20
  33.8 1.3 collective-permute-start.3
  35.1 0.5 collective-permute-done.2
  35.6 4.3 %collective-permute-done.3 = bf16[3,38,256]{2,1,0:T(8,128)(2,1)S(1)} collective-permute-done((bf16[3,38,256]{2,1,0:T(8,128)(2,1)S(1)}, bf16[3,38,256]{2,1,0:T(8,128)(2,1)S(1)}, u32[]{:S(2)}, u32[]{:S(2)}) %collective-permute-start.3) | collective-permute-done | bytes 58400 | tf_op jit(solution)/shard_map/ppermute | solution.py:22
  39.9 0.4 maximum_maximum_fusion
  40.3 8.8 %add_convert_fusion.2 = bf16[32,32,256]{2,1,0:T(8,128)(2,1)} fusion(bf16[32,32,256]{2,1,0:T(8,128)(2,1)S(1)} %fusion.34, bf16[32,3,256]{2,1,0:T(4,128)(2,1)S(1)} %collective-permute-done.1, bf16[32,3,256]{2,1,0:T(4,128)(2,1)S(1)} %collective-permute-done, bf16[35,38,256]{2,1,0:T(8,128)(2,1)S(1)} %get-tuple-element.14, ...), kind=kLoop, calls=%fused_computation.61 | loop fusion | flops 43515904 | bytes 23218176 | tf_op jit(solution)/shard_map/convert_element_type | solution.py:63
  49.3 0.7 constant_dynamic-slice_fusion.6
  50.0 0.1 copy-done.2
  50.2 0.7 constant_dynamic-slice_fusion.8
  50.9 0.7 constant_dynamic-slice_fusion.1
  51.8 0.6 fusion.98
  52.4 6.0 %all-gather.11.cloned.1.call-done = bf16[1024,512]{1,0:T(8,128)(2,1)} async-done(((bf16[1024,256]{1,0:T(8,128)(2,1)}), bf16[1024,512]{1,0:T(8,128)(2,1)}) %all-gather.11.cloned.1.call-update) | async-done | bytes 1048592 | tf_op jit(solution)/shard_map/all_gather | solution.py:110
  58.4 1.6 convert_reduce_fusion.1
  60.0 41.9 %all-gather.17.cloned.1.call-done = bf16[1,4096,128]{2,1,0:T(8,128)(2,1)} async-done(((bf16[1,512,128]{2,1,0:T(8,128)(2,1)}), bf16[1,4096,128]{2,1,0:T(8,128)(2,1)}) %all-gather.17.cloned.1.call-update) | async-done | bytes 1048592 | tf_op jit(solution)/shard_map/all_gather | solution.py:70
  101.9 2.3 copy.34
  104.1 38.9 %all-gather.15.cloned.1.call-done = bf16[1,512,1024]{2,1,0:T(8,128)(2,1)} async-done(((bf16[1,64,1024]{2,1,0:T(8,128)(2,1)}), bf16[1,512,1024]{2,1,0:T(8,128)(2,1)}) %all-gather.15.cloned.1.call-update) | async-done | bytes 1048592 | tf_op jit(solution)/shard_map/all_gather | solution.py:70
  143.0 4.5 %fusion.41 = f32[1024,512]{1,0:T(8,128)S(1)} fusion(bf16[512,1024]{1,0:T(8,128)(2,1)} %bitcast.162, f32[1024]{0:T(1024)S(1)} %bitcast.167, bf16[1024,512]{1,0:T(8,128)(2,1)} %all-gather.11.cloned.1.call-done, bf16[1,512,1024]{2,1,0:T(8,128)(2,1)} %all-gather.15.cloned.1.call-done, f32[512]{0:T(512)S(1)} %bitcast.272, f32[512]{0:T(512)S(1)} %bitcast.271, ...), kind=kOutput, calls=%fused_computation.44 | convolution fusion | flops 2161115136 | bytes 5259264 | tf_op jit(solution)/shard_map/th,zhk->tzk/dot_general | solution.py:120
  147.8 1.8 collective-permute-done.4
  149.6 0.2 fusion.47
  149.9 0.6 collective-permute-start.5
  150.5 3.3 %collective-permute-start.6 = (bf16[32,3,256]{2,1,0:T(4,128)(2,1)S(1)}, bf16[32,3,256]{2,1,0:T(4,128)(2,1)S(1)}, u32[]{:S(2)}, u32[]{:S(2)}) collective-permute-start(bf16[32,3,256]{2,1,0:T(4,128)(2,1)S(1)} %get-tuple-element.20), channel_id=1, source_target_pairs={{4,0},{8,4},{12,8},{0,12},{5,1},{9,5},{13,9},{1,13},{6,2},{10,6},{... | collective-permute-start | bytes 147464 | tf_op jit(solution)/shard_map/ppermute | solution.py:22
  153.8 3.3 %collective-permute-done.5 = bf16[32,3,256]{2,1,0:T(4,128)(2,1)S(1)} collective-permute-done((bf16[32,3,256]{2,1,0:T(4,128)(2,1)S(1)}, bf16[32,3,256]{2,1,0:T(4,128)(2,1)S(1)}, u32[]{:S(2)}, u32[]{:S(2)}) %collective-permute-start.5) | collective-permute-done | bytes 49184 | tf_op jit(solution)/shard_map/ppermute | solution.py:20
  157.1 0.5 collective-permute-done.6
  157.6 1.8 collective-permute-start.7
  159.4 1.3 collective-permute-start.8
  160.7 0.3 collective-permute-done.7
  161.1 4.4 %collective-permute-done.8 = bf16[3,38,256]{2,1,0:T(8,128)(2,1)S(1)} collective-permute-done((bf16[3,38,256]{2,1,0:T(8,128)(2,1)S(1)}, bf16[3,38,256]{2,1,0:T(8,128)(2,1)S(1)}, u32[]{:S(2)}, u32[]{:S(2)}) %collective-permute-start.8) | collective-permute-done | bytes 58400 | tf_op jit(solution)/shard_map/ppermute | solution.py:22
  165.5 0.4 maximum_maximum_fusion.1
  165.9 8.8 %add_convert_fusion.1 = bf16[32,32,256]{2,1,0:T(8,128)(2,1)} fusion(bf16[32,32,256]{2,1,0:T(8,128)(2,1)S(1)} %bitcast.155, bf16[32,3,256]{2,1,0:T(4,128)(2,1)S(1)} %collective-permute-done.6, bf16[32,3,256]{2,1,0:T(4,128)(2,1)S(1)} %collective-permute-done.5, bf16[35,38,256]{2,1,0:T(8,128)(2,1)S(1)} %get-tuple-element.10, ...), kind=kLoop, calls=%fused_computation.55 | loop fusion | flops 43515904 | bytes 23218176 | tf_op jit(solution)/shard_map/convert_element_type | solution.py:63
  174.8 0.7 constant_dynamic-slice_fusion.3
  175.5 9.8 %all-gather.21.cloned.1.call-done = bf16[1,4096,128]{2,1,0:T(8,128)(2,1)} async-done(((bf16[1,512,128]{2,1,0:T(8,128)(2,1)}), bf16[1,4096,128]{2,1,0:T(8,128)(2,1)}) %all-gather.21.cloned.1.call-update) | async-done | bytes 1048592 | tf_op jit(solution)/shard_map/all_gather | solution.py:70
  185.3 2.3 copy.36
  187.6 6.9 %all-gather.13.cloned.1.call-done = bf16[1024,512]{1,0:T(8,128)(2,1)} async-done(((bf16[1024,256]{1,0:T(8,128)(2,1)}), bf16[1024,512]{1,0:T(8,128)(2,1)}) %all-gather.13.cloned.1.call-update) | async-done | bytes 1048592 | tf_op jit(solution)/shard_map/all_gather | solution.py:110
  194.5 1.6 convert_reduce_fusion
  196.1 41.8 %all-gather.19.cloned.1.call-done = bf16[1,512,1024]{2,1,0:T(8,128)(2,1)} async-done(((bf16[1,64,1024]{2,1,0:T(8,128)(2,1)}), bf16[1,512,1024]{2,1,0:T(8,128)(2,1)}) %all-gather.19.cloned.1.call-update) | async-done | bytes 1048592 | tf_op jit(solution)/shard_map/all_gather | solution.py:70
  237.9 4.5 %fusion.37 = f32[1024,512]{1,0:T(8,128)S(1)} fusion(bf16[512,1024]{1,0:T(8,128)(2,1)} %bitcast.161, f32[1024]{0:T(1024)S(1)} %bitcast.168, bf16[1024,512]{1,0:T(8,128)(2,1)} %all-gather.13.cloned.1.call-done, bf16[1,512,1024]{2,1,0:T(8,128)(2,1)} %all-gather.19.cloned.1.call-done, f32[512]{0:T(512)S(1)} %bitcast.270, f32[512]{0:T(512)S(1)} %bitcast.269, ...), kind=kOutput, calls=%fused_computation.43 | convolution fusion | flops 2161115136 | bytes 5259264 | tf_op jit(solution)/shard_map/th,zhk->tzk/dot_general | solution.py:120
  242.6 1.9 collective-permute-done.9
  244.5 1.0 add_convert_fusion
  (69 shorter events, 1.2 us)
Async XLA Ops:
  6.5 15.4 %copy-start = (bf16[128,256]{1,0:T(8,128)(2,1)S(1)}, bf16[128,256]{1,0:T(8,128)(2,1)}, u32[]{:S(2)}) copy-start(bf16[128,256]{1,0:T(8,128)(2,1)} %param.18) | copy-start | bytes 196612
  6.5 6.1 %copy-start.4 = (s32[128,128]{1,0:T(8,128)S(1)}, s32[128,128]{1,0:T(8,128)}, u32[]{:S(2)}) copy-start(s32[128,128]{1,0:T(8,128)} %param.15) | copy-start | bytes 196612
  6.5 6.1 %copy-start.5 = (s32[128,128]{1,0:T(8,128)S(1)}, s32[128,128]{1,0:T(8,128)}, u32[]{:S(2)}) copy-start(s32[128,128]{1,0:T(8,128)} %param.16) | copy-start | bytes 196612
  6.5 51.8 %all-gather.11.cloned.1.call-start = ((), (), s32[]{:S(2)}) async-start(), calls=%async_computation | async-start | bytes 1572864 | tf_op jit(solution)/shard_map/all_gather | solution.py:110
  12.6 5.9 %copy-start.13 = (bf16[69,4,4,256]{3,2,1,0:T(4,128)(2,1)S(1)}, bf16[69,4,4,256]{3,2,1,0:T(4,128)(2,1)}, u32[]{:S(2)}) copy-start(bf16[69,4,4,256]{3,2,1,0:T(4,128)(2,1)} %param.17) | copy-start | bytes 1695748
  21.9 5.5 %copy-start.3 = (f32[2,7,7,256]{3,0,2,1:T(2,128)S(1)}, f32[2,7,7,256]{3,0,2,1:T(2,128)}, u32[]{:S(2)}) copy-start(f32[2,7,7,256]{3,0,2,1:T(2,128)} %param.19) | copy-start | bytes 301060
  21.9 13.2 %copy-start.11 = (f32[2,256]{1,0:T(2,128)S(1)}, f32[2,256]{1,0:T(2,128)}, u32[]{:S(2)}) copy-start(f32[2,256]{1,0:T(2,128)} %param.20) | copy-start | bytes 6148
  22.3 7.5 %collective-permute-start = (bf16[32,3,256]{2,1,0:T(4,128)(2,1)S(1)}, bf16[32,3,256]{2,1,0:T(4,128)(2,1)S(1)}, u32[]{:S(2)}, u32[]{:S(2)}) collective-permute-start(bf16[32,3,256]{2,1,0:T(4,128)(2,1)S(1)} %get-tuple-element.21), channel_id=1, source_target_pairs={{0,4},{4,8},{8,12},{12,0},{1,5},{5,9},{9,13},{13,1},{2,6},{6,10},{... | collective-permute-start | bytes 147464 | tf_op jit(solution)/shard_map/ppermute | solution.py:20
  25.4 5.0 %collective-permute-start.1 = (bf16[32,3,256]{2,1,0:T(4,128)(2,1)S(1)}, bf16[32,3,256]{2,1,0:T(4,128)(2,1)S(1)}, u32[]{:S(2)}, u32[]{:S(2)}) collective-permute-start(bf16[32,3,256]{2,1,0:T(4,128)(2,1)S(1)} %get-tuple-element.22), channel_id=1, source_target_pairs={{4,0},{8,4},{12,8},{0,12},{5,1},{9,5},{13,9},{1,13},{6,2},{10,6},{... | collective-permute-start | bytes 147464 | tf_op jit(solution)/shard_map/ppermute | solution.py:22
  30.4 5.3 %collective-permute-start.2 = (bf16[3,38,256]{2,1,0:T(8,128)(2,1)S(1)}, bf16[3,38,256]{2,1,0:T(8,128)(2,1)S(1)}, u32[]{:S(2)}, u32[]{:S(2)}) collective-permute-start(bf16[3,38,256]{2,1,0:T(8,128)(2,1)S(1)} %get-tuple-element.15), channel_id=1, source_target_pairs={{0,2},{1,3},{4,6},{5,7},{8,10},{9,11},{12,14},{13,15},{16,18},{17,... | collective-permute-start | bytes 175112 | tf_op jit(solution)/shard_map/ppermute | solution.py:20
  33.8 6.1 %collective-permute-start.3 = (bf16[3,38,256]{2,1,0:T(8,128)(2,1)S(1)}, bf16[3,38,256]{2,1,0:T(8,128)(2,1)S(1)}, u32[]{:S(2)}, u32[]{:S(2)}) collective-permute-start(bf16[3,38,256]{2,1,0:T(8,128)(2,1)S(1)} %get-tuple-element.16), channel_id=1, source_target_pairs={{2,0},{3,1},{6,4},{7,5},{10,8},{11,9},{14,12},{15,13},{18,16},{19,... | collective-permute-start | bytes 175112 | tf_op jit(solution)/shard_map/ppermute | solution.py:22
  40.3 8.9 %copy-start.1 = (bf16[2,1024,128]{2,1,0:T(8,128)(2,1)S(1)}, bf16[2,1024,128]{2,1,0:T(8,128)(2,1)}, u32[]{:S(2)}) copy-start(bf16[2,1024,128]{2,1,0:T(8,128)(2,1)} %param.25) | copy-start | bytes 1572868
  49.1 1.0 copy-start.2
  49.1 2.6 %copy-start.6 = (f32[2,2048]{1,0:T(2,128)S(1)}, f32[2,2048]{1,0:T(2,128)}, u32[]{:S(2)}) copy-start(f32[2,2048]{1,0:T(2,128)} %param.24) | copy-start | bytes 49156
  49.1 2.6 %copy-start.7 = (f32[2,512]{1,0:T(2,128)S(1)}, f32[2,512]{1,0:T(2,128)}, u32[]{:S(2)}) copy-start(f32[2,512]{1,0:T(2,128)} %param.21) | copy-start | bytes 12292
  49.1 2.6 %copy-start.8 = (f32[2,512]{1,0:T(2,128)S(1)}, f32[2,512]{1,0:T(2,128)}, u32[]{:S(2)}) copy-start(f32[2,512]{1,0:T(2,128)} %param.22) | copy-start | bytes 12292
  49.1 3.2 %copy-start.9 = (f32[2,512]{1,0:T(2,128)S(1)}, f32[2,512]{1,0:T(2,128)}, u32[]{:S(2)}) copy-start(f32[2,512]{1,0:T(2,128)} %param.27) | copy-start | bytes 12292
  49.2 52.7 %all-gather.17.cloned.1.call-start = ((), (), s32[]{:S(2)}) async-start(), calls=%async_computation.3 | async-start | bytes 1179648 | tf_op jit(solution)/shard_map/all_gather | solution.py:70
  50.0 93.0 %all-gather.15.cloned.1.call-start = ((), (), s32[]{:S(2)}) async-start(), calls=%async_computation.2 | async-start | bytes 1179648 | tf_op jit(solution)/shard_map/all_gather | solution.py:70
  50.9 134.4 %all-gather.21.cloned.1.call-start = ((), (), s32[]{:S(2)}) async-start(), calls=%async_computation.5 | async-start | bytes 1179648 | tf_op jit(solution)/shard_map/all_gather | solution.py:70
  51.6 142.9 %all-gather.13.cloned.1.call-start = ((), (), s32[]{:S(2)}) async-start(), calls=%async_computation.1 | async-start | bytes 1572864 | tf_op jit(solution)/shard_map/all_gather | solution.py:110
  143.0 4.7 %copy-start.10 = (f32[2,512]{1,0:T(2,128)S(1)}, f32[2,512]{1,0:T(2,128)}, u32[]{:S(2)}) copy-start(f32[2,512]{1,0:T(2,128)} %param.26) | copy-start | bytes 12292
  147.6 2.0 collective-permute-start.4
  149.9 7.1 %collective-permute-start.5 = (bf16[32,3,256]{2,1,0:T(4,128)(2,1)S(1)}, bf16[32,3,256]{2,1,0:T(4,128)(2,1)S(1)}, u32[]{:S(2)}, u32[]{:S(2)}) collective-permute-start(bf16[32,3,256]{2,1,0:T(4,128)(2,1)S(1)} %get-tuple-element.19), channel_id=1, source_target_pairs={{0,4},{4,8},{8,12},{12,0},{1,5},{5,9},{9,13},{13,1},{2,6},{6,10},{... | collective-permute-start | bytes 147464 | tf_op jit(solution)/shard_map/ppermute | solution.py:20
  150.5 7.1 %collective-permute-start.6 = (bf16[32,3,256]{2,1,0:T(4,128)(2,1)S(1)}, bf16[32,3,256]{2,1,0:T(4,128)(2,1)S(1)}, u32[]{:S(2)}, u32[]{:S(2)}) collective-permute-start(bf16[32,3,256]{2,1,0:T(4,128)(2,1)S(1)} %get-tuple-element.20), channel_id=1, source_target_pairs={{4,0},{8,4},{12,8},{0,12},{5,1},{9,5},{13,9},{1,13},{6,2},{10,6},{... | collective-permute-start | bytes 147464 | tf_op jit(solution)/shard_map/ppermute | solution.py:22
  157.6 3.5 %collective-permute-start.7 = (bf16[3,38,256]{2,1,0:T(8,128)(2,1)S(1)}, bf16[3,38,256]{2,1,0:T(8,128)(2,1)S(1)}, u32[]{:S(2)}, u32[]{:S(2)}) collective-permute-start(bf16[3,38,256]{2,1,0:T(8,128)(2,1)S(1)} %get-tuple-element.11), channel_id=1, source_target_pairs={{0,2},{1,3},{4,6},{5,7},{8,10},{9,11},{12,14},{13,15},{16,18},{17,... | collective-permute-start | bytes 175112 | tf_op jit(solution)/shard_map/ppermute | solution.py:20
  159.4 6.1 %collective-permute-start.8 = (bf16[3,38,256]{2,1,0:T(8,128)(2,1)S(1)}, bf16[3,38,256]{2,1,0:T(8,128)(2,1)S(1)}, u32[]{:S(2)}, u32[]{:S(2)}) collective-permute-start(bf16[3,38,256]{2,1,0:T(8,128)(2,1)S(1)} %get-tuple-element.12), channel_id=1, source_target_pairs={{2,0},{3,1},{6,4},{7,5},{10,8},{11,9},{14,12},{15,13},{18,16},{19,... | collective-permute-start | bytes 175112 | tf_op jit(solution)/shard_map/ppermute | solution.py:22
  174.7 63.1 %copy-start.12 = (f32[1,512]{1,0:T(1,128)S(1)}, f32[1,512]{1,0:T(1,128)}, u32[]{:S(2)}) copy-start(f32[1,512]{1,0:T(1,128)} %get-tuple-element.135) | copy-start | bytes 6148
  174.8 63.1 %all-gather.19.cloned.1.call-start = ((), (), s32[]{:S(2)}) async-start(), calls=%async_computation.4 | async-start | bytes 1179648 | tf_op jit(solution)/shard_map/all_gather | solution.py:70
  242.5 2.0 collective-permute-start.9
Sparse Core Ops, SparseCore 0:
  49.3 9.0 all-gather.10
  60.5 41.3 all-gather.16
  104.0 38.9 all-gather.14
  145.0 40.2 all-gather.20
  186.7 7.7 all-gather.12
  196.5 41.3 all-gather.18

commit v2 on v1

v2 whole, which is shorter than its diff:
```python
import functools

import jax
import jax.numpy as jnp
import numpy as np
from jax import lax
from jax.experimental import pallas as pl
from jax.experimental.pallas import tpu as pltpu
from jax.sharding import PartitionSpec as P

PATCH = 4
KERNEL = 7
BLOCKS = 2
HALO = 3


def embed_tokens(fields, land_sea, orography, embed_weight, class_table):
    var_count, lat_cells, lon_cells = fields.shape
    tok_rows = lat_cells // PATCH
    tok_cols = lon_cells // PATCH
    width = embed_weight.shape[3]
    cell_grid = fields.reshape(var_count, tok_rows, PATCH, tok_cols, PATCH)
    patch_term = jnp.einsum(
        "vrpcq,vpqk->rck", cell_grid, embed_weight, preferred_element_type=jnp.float32
    )
    class_codes = 2 * orography + land_sea
    classes = class_table.shape[0]
    one_hot = (class_codes[..., None] == jnp.arange(classes, dtype=jnp.int32)).astype(jnp.bfloat16)
    class_counts = one_hot.reshape(tok_rows, PATCH, tok_cols, PATCH, classes).sum(axis=(1, 3))
    static_term = jnp.dot(
        class_counts.reshape(tok_rows * tok_cols, classes),
        class_table,
        preferred_element_type=jnp.float32,
    )
    return (
        patch_term + static_term.reshape(tok_rows, tok_cols, width) * (1.0 / (PATCH * PATCH))
    ).astype(jnp.bfloat16)


LEFT = 8
CORNER = 16
DIRECTIONS = tuple(
    (dx, dz) for dx in (-1, 0, 1) for dz in (-1, 0, 1) if (dx, dz) != (0, 0)
)
CORNERS = tuple(d for d in DIRECTIONS if d[0] and d[1])


def edge_maps(rows, cols):
    side = HALO * rows
    total = 2 * side + CORNER * len(CORNERS)
    pack = np.zeros((total, rows * cols), np.float32)
    spread = np.zeros((2, rows + 2 * HALO, LEFT, total), np.float32)
    for way, dz in enumerate((-1, 1)):
        first = cols - HALO if dz > 0 else 0
        lane = LEFT - HALO if dz > 0 else 0
        rim = 0 if dz > 0 else 1
        for c in range(HALO):
            for r in range(rows):
                slot = way * side + c * rows + r
                pack[slot, r * cols + first + c] = 1
                spread[rim, HALO + r, lane + c, slot] = 1
            for k, (dx, kz) in enumerate(CORNERS):
                if kz != dz:
                    continue
                for i in range(HALO):
                    slot = 2 * side + CORNER * k + c * HALO + i
                    r = rows - HALO + i if dx > 0 else i
                    pack[slot, r * cols + first + c] = 1
                    spread[rim, i if dx > 0 else rows + HALO + i, lane + c, slot] = 1
    return pack, spread.reshape(-1, total)


def kernel_body(
    rows,
    cols,
    stream_in,
    pack,
    spread,
    conv_kernel,
    conv_bias,
    norm_gain,
    norm_bias,
    weight_in,
    up_bias,
    down_bias,
    layer_scale,
    out,
    stream,
    edges,
    rim,
    band,
    frame,
    shifted,
    conv_all,
    weights,
    mine,
    outgoing,
    incoming,
    halo_send,
    halo_recv,
    z_send,
    z_recv,
    h_send,
    h_recv,
    conv_send,
    conv_recv,
    part_send,
    part_recv,
):
    lats, lons, grps = lax.axis_size("lat"), lax.axis_size("lon"), lax.axis_size("grp")
    x, z, y, core = (lax.axis_index(n) for n in ("lat", "lon", "grp", "ch"))
    tokens, half = rows * cols, stream.shape[1]
    channels = norm_gain.shape[1]
    hid = weights.shape[2]
    share = weight_in.shape[1]
    side = HALO * rows
    partner = {"ch": 1 - core}
    mesh_ids = pl.DeviceIdType.MESH

    def remote(src, dst, send, recv, device):
        return pltpu.make_async_remote_copy(
            src_ref=src,
            dst_ref=dst,
            send_sem=send,
            recv_sem=recv,
            device_id=device,
            device_id_type=mesh_ids,
        )

    def helper(m):
        name, count, index = (("lat", lats, x), ("grp", grps, y))[m % 2]
        if share % (16 * count):
            return name, 1, 0
        return name, count, index

    def piece(m, owner, index):
        count = helper(m)[1]
        part = share // count
        start = pl.multiple_of(owner * share + index * part, 16)
        return weights.at[m, pl.ds(start, part)]

    def z_copy(m, dz):
        ref = piece(m, z, helper(m)[2])
        return remote(
            ref, ref, z_send.at[m, dz - 1], z_recv.at[m, dz - 1], {"lon": lax.rem(z + dz, lons)}
        )

    def z_landed(m, dz):
        ref = piece(m, lax.rem(z - dz + lons, lons), helper(m)[2])
        return remote(
            ref, ref, z_send.at[m, dz - 1], z_recv.at[m, dz - 1], {"lon": lax.rem(z + dz, lons)}
        )

    def h_copy(m, dz, dh, back):
        name, count, index = helper(m)
        owner = lax.rem(z - dz + lons, lons)
        ref = piece(m, owner, lax.rem(index - dh + count, count) if back else index)
        return remote(
            ref,
            ref,
            h_send.at[m, dz - 1, dh - 1],
            h_recv.at[m, dz - 1, dh - 1],
            {name: lax.rem(index + dh, count)},
        )

    def send_weights(layer):
        for dz in range(1, lons):
            for m in (2 * layer, 2 * layer + 1):
                z_copy(m, dz).start()

    def pass_on(layer, dz):
        for m in (2 * layer, 2 * layer + 1):
            z_landed(m, dz).wait_recv()
            for dh in range(1, helper(m)[1]):
                h_copy(m, dz, dh, False).start()

    def finish_weights(layer):
        for m in (2 * layer, 2 * layer + 1):
            for dz in range(1, lons):
                z_copy(m, dz).wait_send()
                for dh in range(1, helper(m)[1]):
                    h_copy(m, dz, dh, False).wait_send()
                    h_copy(m, dz, dh, True).wait_recv()

    def halo_copy(layer, k):
        dx, dz = DIRECTIONS[k]
        if dz == 0:
            src = stream.at[pl.ds((rows - HALO if dx > 0 else 0) * cols, HALO * cols)]
            dst = band.at[layer, 0 if dx > 0 else 1]
        else:
            if dx == 0:
                where = pl.ds(0 if dz < 0 else side, side)
            else:
                where = pl.ds(2 * side + CORNER * CORNERS.index((dx, dz)), CORNER)
            src, dst = edges.at[layer, where], rim.at[layer, where]
        device = {"lat": x + dx, "lon": lax.rem(z + dz + lons, lons)}
        return remote(src, dst, halo_send.at[layer, k], halo_recv.at[layer, k], device)

    def each_halo(layer, act, arriving):
        for k, (dx, _) in enumerate(DIRECTIONS):
            where = x - dx if arriving else x + dx
            if dx == 0:
                act(halo_copy(layer, k))
            else:

                @pl.when((where >= 0) & (where < lats))
                def _():
                    act(halo_copy(layer, k))

    barrier = pltpu.get_barrier_semaphore()

    def greet(device):
        pl.semaphore_signal(barrier, inc=1, device_id=device, device_id_type=mesh_ids)

    rim[...] = jnp.zeros_like(rim)
    band[...] = jnp.zeros_like(band)
    for k, (dx, dz) in enumerate(DIRECTIONS):
        device = {"lat": x + dx, "lon": lax.rem(z + dz + lons, lons)}
        if dx == 0:
            greet(device)
        else:

            @pl.when((x + dx >= 0) & (x + dx < lats))
            def _():
                greet(device)

    for dz in range(1, lons):
        greet({"lon": lax.rem(z + dz, lons)})
    for dx in range(1, lats):
        greet({"lat": lax.rem(x + dx, lats)})
    for dy in range(1, grps):
        greet({"grp": lax.rem(y + dy, grps)})
    greet(partner)
    owed = 2 + (lons - 1) + (lats - 1) + (grps - 1) + 1
    inner = (x > 0).astype(jnp.int32) + (x < lats - 1).astype(jnp.int32)
    stream[...] = stream_in[...]
    mine_rows = pl.ds(pl.multiple_of(z * share, 16), share)
    for m in range(2 * BLOCKS):
        weights[m, mine_rows] = weight_in[m]

    for layer in range(BLOCKS):
        edges[layer] = jnp.dot(
            pack[...], stream[...], preferred_element_type=jnp.float32
        ).astype(jnp.bfloat16)
        if layer == 0:
            pl.semaphore_wait(barrier, owed + 3 * inner)
        each_halo(layer, lambda c: c.start(), False)
        if layer == 0:
            send_weights(0)
        frame[HALO : HALO + rows, LEFT : LEFT + cols] = (
            stream[...].astype(jnp.float32).reshape(rows, cols, half)
        )
        each_halo(layer, lambda c: c.wait_recv(), True)
        ends = jnp.dot(spread[...], rim[layer], preferred_element_type=jnp.float32).reshape(
            2, rows + 2 * HALO, LEFT, half
        )
        frame[:, :LEFT] = ends[0]
        frame[:, LEFT + cols :] = ends[1]
        for end, first in ((0, 0), (1, HALO + rows)):
            frame[first : first + HALO, LEFT : LEFT + cols] = (
                band[layer, end].astype(jnp.float32).reshape(HALO, cols, half)
            )

        def shift_row(r, _):
            line = frame[r]
            for e in range(KERNEL):
                first = LEFT - HALO + e
                shifted[e, r] = line[first : first + cols]
            return 0

        lax.fori_loop(0, rows + 2 * HALO, shift_row, 0)

        def conv_row(i, _):
            total = jnp.broadcast_to(conv_bias[layer, 0], (cols, half))
            for a in range(KERNEL):
                for e in range(KERNEL):
                    total = total + shifted[e, i + a] * conv_kernel[layer, a, e]
            at = pl.ds(pl.multiple_of(i * cols, 16), cols)
            conv_all[layer, core, at] = total.astype(jnp.bfloat16)
            return 0

        quarters = 4
        step = rows // quarters
        order = [1, lons - 1] + list(range(2, lons - 1))
        order = order[: lons - 1]

        def conv_copy(q):
            at = pl.ds(q * step * cols, step * cols)
            ref = conv_all.at[layer, core, at]
            return remote(ref, ref, conv_send.at[layer, q], conv_recv.at[layer, q], partner)

        def conv_landed(q):
            at = pl.ds(q * step * cols, step * cols)
            ref = conv_all.at[layer, 1 - core, at]
            return remote(ref, ref, conv_send.at[layer, q], conv_recv.at[layer, q], partner)

        for q in range(quarters):
            lax.fori_loop(q * step, (q + 1) * step, conv_row, 0)
            conv_copy(q).start()
            if q:
                cut = len(order)
                for dz in order[(q - 1) * cut // 3 : q * cut // 3]:
                    pass_on(layer, dz)
        if layer + 1 < BLOCKS:
            send_weights(layer + 1)
        finish_weights(layer)
        for q in range(quarters):
            conv_landed(q).wait_recv()
            conv_copy(q).wait_send()
        each_halo(layer, lambda c: c.wait_send(), False)

        chunk = step * cols

        def part_copy(c):
            at = pl.ds(pl.multiple_of(c * chunk, 16), chunk)
            return remote(
                outgoing.at[layer, at],
                incoming.at[layer, at],
                part_send.at[layer, c],
                part_recv.at[layer, c],
                partner,
            )

        up, down = 2 * layer, 2 * layer + 1
        own = pl.ds(pl.multiple_of(core * half, 128), half)
        other = pl.ds(pl.multiple_of((1 - core) * half, 128), half)
        contract = (((1,), (1,)), ((), ()))

        def ffn(c, _):
            at = pl.ds(pl.multiple_of(c * chunk, 16), chunk)
            conv_f = jnp.concatenate(
                [conv_all[layer, 0, at], conv_all[layer, 1, at]], axis=1
            ).astype(jnp.float32)
            average = jnp.sum(conv_f, axis=1, keepdims=True) / channels
            variance = (
                jnp.sum(conv_f * conv_f, axis=1, keepdims=True) / channels - average * average
            )
            normed = (
                (conv_f - average) * lax.rsqrt(variance + 1e-06) * norm_gain[layer : layer + 1]
                + norm_bias[layer : layer + 1]
            ).astype(jnp.bfloat16)
            pre = jnp.dot(normed, weights[up], preferred_element_type=jnp.float32)
            pre = pre + up_bias[layer : layer + 1, pl.ds(pl.multiple_of(core * hid, 128), hid)]
            hidden = jax.nn.gelu(pre, approximate=True).astype(jnp.bfloat16)
            outgoing[layer, at] = lax.dot_general(
                hidden, weights[down, other], contract, preferred_element_type=jnp.float32
            ).astype(jnp.bfloat16)
            part_copy(c).start()
            mine[at] = lax.dot_general(
                hidden, weights[down, own], contract, preferred_element_type=jnp.float32
            )
            return 0

        lax.fori_loop(0, quarters, ffn, 0)

        def merge(c, _):
            at = pl.ds(pl.multiple_of(c * chunk, 16), chunk)
            part_copy(c).wait_recv()
            update = mine[at] + incoming[layer, at].astype(jnp.float32)
            fresh = stream[at].astype(jnp.float32) + layer_scale[layer : layer + 1, own] * (
                update + down_bias[layer : layer + 1, own]
            )
            if layer + 1 < BLOCKS:
                stream[at] = fresh.astype(jnp.bfloat16)
            else:
                out[at] = fresh.astype(jnp.bfloat16)
            part_copy(c).wait_send()
            return 0

        lax.fori_loop(0, quarters, merge, 0)


def body(
    fields,
    land_sea,
    orography,
    embed_weight,
    class_table,
    conv_kernel,
    conv_bias,
    norm_gain,
    norm_bias,
    up_proj,
    up_bias,
    down_proj,
    down_bias,
    layer_scale,
):
    var_count, lat_cells, lon_cells = fields.shape
    rows = lat_cells // PATCH
    cols = lon_cells // PATCH
    tokens = rows * cols
    channels = norm_gain.shape[1]
    half = embed_weight.shape[3]
    hid = up_proj.shape[2]
    lats, lons, grps = lax.axis_size("lat"), lax.axis_size("lon"), lax.axis_size("grp")
    stream = embed_tokens(fields, land_sea, orography, embed_weight, class_table)
    pack, spread = edge_maps(rows, cols)
    packed = pack.shape[0]
    weight_in = jnp.stack(
        [w for b in range(BLOCKS) for w in (up_proj[b], down_proj[b].T)]
    )
    arrays = 2 * BLOCKS
    helpers = max(lats, grps, 2) - 1
    vmem = pl.BlockSpec(memory_space=pltpu.VMEM)
    dma = pltpu.SemaphoreType.DMA
    result = pl.pallas_call(
        functools.partial(kernel_body, rows, cols),
        out_shape=jax.ShapeDtypeStruct((tokens, half), jnp.bfloat16),
        in_specs=[vmem] * 11,
        out_specs=vmem,
        scratch_shapes=[
            pltpu.VMEM((tokens, half), jnp.bfloat16),
            pltpu.VMEM((BLOCKS, packed, half), jnp.bfloat16),
            pltpu.VMEM((BLOCKS, packed, half), jnp.bfloat16),
            pltpu.VMEM((BLOCKS, 2, HALO * cols, half), jnp.bfloat16),
            pltpu.VMEM((rows + 2 * HALO, cols + 2 * LEFT, half), jnp.float32),
            pltpu.VMEM((KERNEL, rows + 2 * HALO, cols, half), jnp.float32),
            pltpu.VMEM((BLOCKS, 2, tokens, half), jnp.bfloat16),
            pltpu.VMEM((arrays, channels, hid), jnp.bfloat16),
            pltpu.VMEM((tokens, half), jnp.float32),
            pltpu.VMEM((BLOCKS, tokens, half), jnp.bfloat16),
            pltpu.VMEM((BLOCKS, tokens, half), jnp.bfloat16),
            dma((BLOCKS, len(DIRECTIONS))),
            dma((BLOCKS, len(DIRECTIONS))),
            dma((arrays, lons - 1)),
            dma((arrays, lons - 1)),
            dma((arrays, lons - 1, helpers)),
            dma((arrays, lons - 1, helpers)),
            dma((BLOCKS, 4)),
            dma((BLOCKS, 4)),
            dma((BLOCKS, 4)),
            dma((BLOCKS, 4)),
        ],
        compiler_params=pltpu.CompilerParams(
            collective_id=0, has_side_effects=True, vmem_limit_bytes=48 * 1024 * 1024
        ),
    )(
        stream.reshape(tokens, half),
        jnp.asarray(pack, jnp.bfloat16),
        jnp.asarray(spread, jnp.bfloat16),
        conv_kernel,
        conv_bias.reshape(BLOCKS, 1, half),
        norm_gain,
        norm_bias,
        weight_in,
        up_bias,
        down_bias,
        layer_scale,
    )
    return result.reshape(rows, cols, half)


def solution(mesh):
    in_specs = (
        P(None, ("grp", "lat"), "lon"),
        P("lat", "lon"),
        P("lat", "lon"),
        P(None, None, None, "ch"),
        P(None, "ch"),
        P(None, None, None, "ch"),
        P(None, "ch"),
        P(),
        P(),
        P(None, "lon", "ch"),
        P(),
        P(None, "ch", "lon"),
        P(),
        P(),
    )
    out_specs = P(("grp", "lat"), "lon", "ch")
    return jax.shard_map(body, mesh=mesh, in_specs=in_specs, out_specs=out_specs, check_vma=False)
```

time: 253 us -> 96.5 us (0.38)
  the two profiles are of different devices: /device:TPU:0 before, /device:TPU:17 now
where the time goes in v2:
time: 96.5 us; the launch traced here: 96.2 us
  Pallas kernels  76.1 us (79%)
  local copies, waits for them, and re-layouts  13.2 us (14%)
  matrix products  3.68 us (4%)
  other arithmetic  2.97 us (3%)
    pallas_call x1, Pallas kernels, body(): pl.pallas_call(functools.partial(kernel_body, rows, cols), out_shape=jax....  76.1 us
    unnamed x29, local copies, waits for them, and re-layouts  8.08 us
    dot_general x1, matrix products, embed_tokens(): jnp.einsum('vrpcq,vpqk->rck', cell_grid, embed_weight, preferred_element_...  3.41 us
    eq x2, local copies, waits for them, and re-layouts, embed_tokens(): class_codes[..., None] == jnp.arange(classes, dtype=jnp.int32)  2.99 us
    reduce_sum x1, other arithmetic, embed_tokens(): one_hot.reshape(tok_rows, PATCH, tok_cols, PATCH, classes).sum(axis=(1, 3))  2.82 us

profile of v2, /device:TPU:17, one launch (start us, length us, event | category | flops | bytes accessed | tf_op | source)
XLA Modules:
  0.0 96.2 jit_solution(9057888097378410926)
XLA Ops:
  0.0 0.0 copy-start
  0.0 0.0 copy-start.11
  0.0 6.0 %copy.28 = bf16[69,128,128]{0,2,1:T(8,128)(2,1)} copy(bf16[69,128,128]{2,1,0:T(8,128)(2,1)} %param.16) | data formatting | bytes 4521984 | tf_op args[0]
  6.0 0.0 copy-done.11
  6.0 0.0 copy-start.8
  6.0 0.0 copy-start.9
  6.0 3.4 %fusion.4 = f32[32,32,256]{2,1,0:T(8,128)S(1)} fusion(bf16[69,32,4,32,4]{0,4,3,2,1:T(4,128)(2,1)} %bitcast.26, bf16[69,4,4,256]{3,2,1,0:T(4,128)(2,1)S(1)} %copy-done.11), kind=kOutput, calls=%fused_computation.5 | convolution fusion | flops 578813952 | bytes 3874816 | tf_op jit(solution)/shard_map/vrpcq,vpqk->rck/dot_general | solution.py:23
  9.5 0.0 copy-done.8
  9.5 0.0 copy-done.9
  9.5 0.0 copy-start.10
  9.5 2.1 %eq.16 = s32[32,4,32,4]{3,2,1,0:T(8,128)S(1)} reshape(s32[128,128]{1,0:T(8,128)S(1)} %multiply_add_fusion) | data formatting | bytes 131072 | tf_op jit(solution)/shard_map/eq | solution.py:28
  11.7 0.8 copy.31
  12.5 0.0 copy-start.1
  12.5 0.0 copy-start.2
  12.5 0.0 copy-start.3
  12.5 0.0 copy-start.4
  12.5 0.0 copy-start.5
  12.6 0.0 copy-start.6
  12.6 0.0 copy-start.7
  12.6 2.8 %fusion.1 = bf16[32,32,128]{2,1,0:T(8,128)(2,1)S(1)} fusion(s32[32,4,32,4]{2,3,1,0:T(4,128)S(1)} %copy.31), kind=kLoop, calls=%fused_computation.2 | loop fusion | flops 6160384 | bytes 327680 | tf_op jit(solution)/shard_map/reduce_sum | solution.py:29
  15.4 0.0 copy-done
  15.4 0.3 fusion.8
  15.7 0.9 copy.34.conv_kernel
  16.6 0.0 copy-done.10
  16.6 1.1 %fusion.13 = (bf16[1,1024,128]{2,1,0:T(8,128)(2,1)S(1)}, bf16[1,1024,128]{2,1,0:T(8,128)(2,1)S(1)}) fusion(bf16[2,1024,128]{2,1,0:T(8,128)(2,1)} %param.27), kind=kLoop, calls=%fused_computation.15 | loop fusion | bytes 1048576 | tf_op jit(solution)/shard_map/slice | solution.py:401
  17.7 0.1 copy.37
  17.9 1.1 %fusion.12 = (bf16[1,128,1024]{2,1,0:T(8,128)(2,1)S(1)}, bf16[1,128,1024]{2,1,0:T(8,128)(2,1)S(1)}) fusion(bf16[2,128,1024]{2,1,0:T(8,128)(2,1)} %param.25), kind=kLoop, calls=%fused_computation.14 | loop fusion | bytes 1048576 | tf_op jit(solution)/shard_map/slice | solution.py:401
  18.9 0.1 copy.36
  19.1 0.1 pad_maximum_fusion.weight_in
  19.2 0.0 copy-done.1
  19.2 0.0 copy-done.2
  19.2 0.0 copy-done.3
  19.3 0.0 copy-done.4
  19.3 0.0 copy-done.5
  19.3 0.0 copy-done.6
  19.3 0.0 copy-done.7
  19.3 76.1 %shard_map.154 = bf16[1024,256]{1,0:T(8,128)(2,1)S(1)} custom-call(bf16[1024,256]{1,0:T(8,128)(2,1)S(1)} %bitcast.25, bf16[256,1024]{1,0:T(8,128)(2,1)S(1)} %copy-done.1, bf16[608,256]{1,0:T(8,128)(2,1)S(1)} %copy-done.2, f32[2,7,7,256]{3,2,1,0:T(8,128)S(1)} %copy.34.conv_kernel, f32[2,1,256]{2,1,0:T(1,128)S(1)} %reshape.22.conv_bias, ...), custom_call_target="tpu_custom_call" | custom-call | tf_op jit(solution)/shard_map/pallas_call | solution.py:407
  95.4 0.8 copy.47
  (2 shorter events, 0.0 us)
Async XLA Ops:
  0.0 15.4 %copy-start = (bf16[128,256]{1,0:T(8,128)(2,1)S(1)}, bf16[128,256]{1,0:T(8,128)(2,1)}, u32[]{:S(2)}) copy-start(bf16[128,256]{1,0:T(8,128)(2,1)} %param.20) | copy-start | bytes 196612
  0.0 6.0 %copy-start.11 = (bf16[69,4,4,256]{3,2,1,0:T(4,128)(2,1)S(1)}, bf16[69,4,4,256]{3,2,1,0:T(4,128)(2,1)}, u32[]{:S(2)}) copy-start(bf16[69,4,4,256]{3,2,1,0:T(4,128)(2,1)} %param.19) | copy-start | bytes 1695748
  6.0 3.4 %copy-start.8 = (s32[128,128]{1,0:T(8,128)S(1)}, s32[128,128]{1,0:T(8,128)}, u32[]{:S(2)}) copy-start(s32[128,128]{1,0:T(8,128)} %param.17) | copy-start | bytes 196612
  6.0 3.4 %copy-start.9 = (s32[128,128]{1,0:T(8,128)S(1)}, s32[128,128]{1,0:T(8,128)}, u32[]{:S(2)}) copy-start(s32[128,128]{1,0:T(8,128)} %param.18) | copy-start | bytes 196612
  9.5 7.1 %copy-start.10 = (f32[2,256]{1,0:T(2,128)S(1)}, f32[2,256]{1,0:T(2,128)}, u32[]{:S(2)}) copy-start(f32[2,256]{1,0:T(2,128)} %param.22) | copy-start | bytes 6148
  12.5 6.7 %copy-start.1 = (bf16[256,1024]{1,0:T(8,128)(2,1)S(1)}, bf16[256,1024]{1,0:T(8,128)(2,1)}, u32[]{:S(2)}) copy-start(bf16[256,1024]{1,0:T(8,128)(2,1)} %constant.11.clone.pack) | copy-start | bytes 1572868
  12.5 6.7 %copy-start.2 = (bf16[608,256]{1,0:T(8,128)(2,1)S(1)}, bf16[608,256]{1,0:T(8,128)(2,1)}, u32[]{:S(2)}) copy-start(bf16[608,256]{1,0:T(8,128)(2,1)} %constant.12.clone.spread) | copy-start | bytes 933892
  12.5 6.7 %copy-start.3 = (f32[2,2048]{1,0:T(2,128)S(1)}, f32[2,2048]{1,0:T(2,128)}, u32[]{:S(2)}) copy-start(f32[2,2048]{1,0:T(2,128)} %up_bias.1) | copy-start | bytes 49156
  12.5 6.7 %copy-start.4 = (f32[2,512]{1,0:T(2,128)S(1)}, f32[2,512]{1,0:T(2,128)}, u32[]{:S(2)}) copy-start(f32[2,512]{1,0:T(2,128)} %norm_gain.1) | copy-start | bytes 12292
  12.5 6.7 %copy-start.5 = (f32[2,512]{1,0:T(2,128)S(1)}, f32[2,512]{1,0:T(2,128)}, u32[]{:S(2)}) copy-start(f32[2,512]{1,0:T(2,128)} %norm_bias.1) | copy-start | bytes 12292
  12.6 6.7 %copy-start.6 = (f32[2,512]{1,0:T(2,128)S(1)}, f32[2,512]{1,0:T(2,128)}, u32[]{:S(2)}) copy-start(f32[2,512]{1,0:T(2,128)} %down_bias.1) | copy-start | bytes 12292
  12.6 6.7 %copy-start.7 = (f32[2,512]{1,0:T(2,128)S(1)}, f32[2,512]{1,0:T(2,128)}, u32[]{:S(2)}) copy-start(f32[2,512]{1,0:T(2,128)} %layer_scale.1) | copy-start | bytes 12292

commit v3 on v2

--- a/solution.py
+++ b/solution.py
@@ -14,27 +14,14 @@
 HALO = 3
 
 
-def embed_tokens(fields, land_sea, orography, embed_weight, class_table):
+def token_cells(fields, land_sea, orography):
     var_count, lat_cells, lon_cells = fields.shape
-    tok_rows = lat_cells // PATCH
-    tok_cols = lon_cells // PATCH
-    width = embed_weight.shape[3]
-    cell_grid = fields.reshape(var_count, tok_rows, PATCH, tok_cols, PATCH)
-    patch_term = jnp.einsum(
-        "vrpcq,vpqk->rck", cell_grid, embed_weight, preferred_element_type=jnp.float32
-    )
-    class_codes = 2 * orography + land_sea
-    classes = class_table.shape[0]
-    one_hot = (class_codes[..., None] == jnp.arange(classes, dtype=jnp.int32)).astype(jnp.bfloat16)
-    class_counts = one_hot.reshape(tok_rows, PATCH, tok_cols, PATCH, classes).sum(axis=(1, 3))
-    static_term = jnp.dot(
-        class_counts.reshape(tok_rows * tok_cols, classes),
-        class_table,
-        preferred_element_type=jnp.float32,
-    )
-    return (
-        patch_term + static_term.reshape(tok_rows, tok_cols, width) * (1.0 / (PATCH * PATCH))
-    ).astype(jnp.bfloat16)
+    rows, cols = lat_cells // PATCH, lon_cells // PATCH
+    grid = fields.reshape(var_count, rows, PATCH, cols, PATCH)
+    patches = grid.transpose(2, 4, 1, 3, 0).reshape(PATCH * PATCH, rows * cols, var_count)
+    codes = (2 * orography + land_sea).reshape(rows, PATCH, cols, PATCH)
+    codes = codes.transpose(0, 2, 1, 3).reshape(rows * cols, PATCH * PATCH)
+    return patches, codes
 
 
 LEFT = 8
@@ -73,14 +60,18 @@
 def kernel_body(
     rows,
     cols,
-    stream_in,
+    patches,
+    codes,
+    embed_weight,
+    class_table,
     pack,
     spread,
     conv_kernel,
     conv_bias,
     norm_gain,
     norm_bias,
-    weight_in,
+    up_proj,
+    down_proj,
     up_bias,
     down_bias,
     layer_scale,
@@ -112,7 +103,7 @@
     tokens, half = rows * cols, stream.shape[1]
     channels = norm_gain.shape[1]
     hid = weights.shape[2]
-    share = weight_in.shape[1]
+    share = up_proj.shape[1]
     side = HALO * rows
     partner = {"ch": 1 - core}
     mesh_ids = pl.DeviceIdType.MESH
@@ -233,24 +224,46 @@
     greet(partner)
     owed = 2 + (lons - 1) + (lats - 1) + (grps - 1) + 1
     inner = (x > 0).astype(jnp.int32) + (x < lats - 1).astype(jnp.int32)
-    stream[...] = stream_in[...]
     mine_rows = pl.ds(pl.multiple_of(z * share, 16), share)
-    for m in range(2 * BLOCKS):
-        weights[m, mine_rows] = weight_in[m]
+    for b in range(BLOCKS):
+        weights[2 * b, mine_rows] = up_proj[b]
+        weights[2 * b + 1, mine_rows] = down_proj[b].T
+    pl.semaphore_wait(barrier, owed + 3 * inner)
+    send_weights(0)
+
+    piece_rows = tokens // 4
+
+    def embed(c, _):
+        at = pl.ds(pl.multiple_of(c * piece_rows, 16), piece_rows)
+        classes = class_table.shape[0]
+        ids = lax.broadcasted_iota(jnp.int32, (piece_rows, classes), 1)
+        cells = codes[at]
+        counts = jnp.zeros((piece_rows, classes), jnp.float32)
+        for s in range(PATCH * PATCH):
+            counts = counts + jnp.where(cells[:, s : s + 1] == ids, 1.0, 0.0)
+        total = jnp.dot(
+            counts.astype(jnp.bfloat16), class_table[...], preferred_element_type=jnp.float32
+        ) * (1.0 / (PATCH * PATCH))
+        for s in range(PATCH * PATCH):
+            total = total + jnp.dot(
+                patches[s, at], embed_weight[s], preferred_element_type=jnp.float32
+            )
+        stream[at] = total.astype(jnp.bfloat16)
+        return 0
+
+    lax.fori_loop(0, 4, embed, 0)
 
     for layer in range(BLOCKS):
         edges[layer] = jnp.dot(
             pack[...], stream[...], preferred_element_type=jnp.float32
         ).astype(jnp.bfloat16)
-        if layer == 0:
-            pl.semaphore_wait(barrier, owed + 3 * inner)
         each_halo(layer, lambda c: c.start(), False)
-        if layer == 0:
-            send_weights(0)
         frame[HALO : HALO + rows, LEFT : LEFT + cols] = (
             stream[...].astype(jnp.float32).reshape(rows, cols, half)
         )
         each_halo(layer, lambda c: c.wait_recv(), True)
+        if layer + 1 < BLOCKS:
+            send_weights(layer + 1)
         ends = jnp.dot(spread[...], rim[layer], preferred_element_type=jnp.float32).reshape(
             2, rows + 2 * HALO, LEFT, half
         )
@@ -301,8 +314,6 @@
                 cut = len(order)
                 for dz in order[(q - 1) * cut // 3 : q * cut // 3]:
                     pass_on(layer, dz)
-        if layer + 1 < BLOCKS:
-            send_weights(layer + 1)
         finish_weights(layer)
         for q in range(quarters):
             conv_landed(q).wait_recv()
@@ -394,12 +405,9 @@
     half = embed_weight.shape[3]
     hid = up_proj.shape[2]
     lats, lons, grps = lax.axis_size("lat"), lax.axis_size("lon"), lax.axis_size("grp")
-    stream = embed_tokens(fields, land_sea, orography, embed_weight, class_table)
+    patches, codes = token_cells(fields, land_sea, orography)
     pack, spread = edge_maps(rows, cols)
     packed = pack.shape[0]
-    weight_in = jnp.stack(
-        [w for b in range(BLOCKS) for w in (up_proj[b], down_proj[b].T)]
-    )
     arrays = 2 * BLOCKS
     helpers = max(lats, grps, 2) - 1
     vmem = pl.BlockSpec(memory_space=pltpu.VMEM)
@@ -407,7 +415,7 @@
     result = pl.pallas_call(
         functools.partial(kernel_body, rows, cols),
         out_shape=jax.ShapeDtypeStruct((tokens, half), jnp.bfloat16),
-        in_specs=[vmem] * 11,
+        in_specs=[vmem] * 15,
         out_specs=vmem,
         scratch_shapes=[
             pltpu.VMEM((tokens, half), jnp.bfloat16),
@@ -436,14 +444,18 @@
             collective_id=0, has_side_effects=True, vmem_limit_bytes=48 * 1024 * 1024
         ),
     )(
-        stream.reshape(tokens, half),
+        patches,
+        codes,
+        embed_weight.transpose(1, 2, 0, 3).reshape(PATCH * PATCH, var_count, half),
+        class_table,
         jnp.asarray(pack, jnp.bfloat16),
         jnp.asarray(spread, jnp.bfloat16),
         conv_kernel,
         conv_bias.reshape(BLOCKS, 1, half),
         norm_gain,
         norm_bias,
-        weight_in,
+        up_proj,
+        down_proj,
         up_bias,
         down_bias,
         layer_scale,

time: 96.5 us -> 110 us (1.14)
  the two profiles are of different devices: /device:TPU:17 before, /device:TPU:0 now
where the time goes in v3:
time: 110 us
  Pallas kernels  90.5 us (82%)
  local copies, waits for them, and re-layouts  19.5 us (18%)
    pallas_call x1, Pallas kernels, body(): pl.pallas_call(functools.partial(kernel_body, rows, cols), out_shape=jax....  90.5 us
    unnamed x31, local copies, waits for them, and re-layouts  6.89 us
    transpose x1, local copies, waits for them, and re-layouts, token_cells(): grid.transpose(2, 4, 1, 3, 0).reshape(PATCH * PATCH, rows * cols, var_count)  4.94 us
    reshape x1, local copies, waits for them, and re-layouts, token_cells(): codes = (2 * orography + land_sea).reshape(rows, PATCH, cols, PATCH)  3.5 us
    transpose x1, local copies, waits for them, and re-layouts, token_cells(): codes = codes.transpose(0, 2, 1, 3).reshape(rows * cols, PATCH * PATCH)  2.55 us

profile of v3, /device:TPU:0, one launch (start us, length us, event | category | flops | bytes accessed | tf_op | source)
XLA Modules:
  0.0 110.2 jit_solution(15663300654157478054)
XLA Ops:
  0.0 6.0 %copy.21 = bf16[69,128,128]{0,2,1:T(8,128)(2,1)} copy(bf16[69,128,128]{2,1,0:T(8,128)(2,1)} %param.16) | data formatting | bytes 4521984 | tf_op args[0]
  6.0 0.0 copy-start.11
  6.0 0.0 copy-start.12
  6.0 4.9 %copy.22 = bf16[4,4,32,32,69]{4,3,2,1,0:T(8,128)(2,1)} copy(bf16[4,4,32,32,69]{4,1,3,0,2:T(4,128)(2,1)} %bitcast.15) | data formatting | bytes 4521984 | tf_op jit(solution)/shard_map/transpose | solution.py:21
  11.0 0.0 copy-start.10
  11.0 0.0 copy-start.13
  11.0 0.0 copy-start
  11.0 0.0 copy-start.1
  11.0 0.0 copy-start.2
  11.0 0.0 copy-start.3
  11.0 0.0 copy-start.4
  11.0 0.0 copy-start.5
  11.0 0.0 copy-start.6
  11.0 0.0 copy-start.7
  11.0 0.0 copy-start.8
  11.0 0.0 copy-start.9
  11.1 0.0 copy-done.11
  11.1 0.0 copy-done.12
  11.1 3.5 %reshape.23 = s32[32,4,32,4]{3,2,1,0:T(8,128)} reshape(s32[128,128]{1,0:T(8,128)S(1)} %multiply_add_fusion) | data formatting | bytes 131072 | tf_op jit(solution)/shard_map/reshape | solution.py:22
  14.6 2.5 %copy.23 = s32[32,32,4,4]{1,0,3,2:T(8,128)S(1)} copy(s32[32,32,4,4]{3,1,2,0:T(8,128)} %bitcast.16) | data formatting | bytes 131072 | tf_op jit(solution)/shard_map/transpose | solution.py:23
  17.1 0.1 reshape.24
  17.3 0.2 copy.25.codes
  17.5 1.2 %copy.24 = bf16[4,4,69,256]{3,2,1,0:T(8,128)(2,1)S(1)} copy(bf16[4,4,69,256]{3,1,0,2:T(4,128)(2,1)} %bitcast.17) | data formatting | bytes 1130496 | tf_op jit(solution)/shard_map/transpose | solution.py:449
  18.7 0.0 copy-done.10
  18.8 0.0 copy-done.13
  18.8 0.0 copy-done
  18.8 0.0 copy-done.1
  18.8 0.0 copy-done.2
  18.8 0.0 copy-done.3
  18.8 0.0 copy-done.4
  18.8 0.0 copy-done.5
  18.9 0.0 copy-done.6
  18.9 0.0 copy-done.7
  18.9 0.0 copy-done.8
  18.9 0.0 copy-done.9
  18.9 90.5 %shard_map.154 = bf16[1024,256]{1,0:T(8,128)(2,1)S(1)} custom-call(bf16[16,1024,69]{2,1,0:T(8,128)(2,1)} %bitcast.14, s32[1024,16]{1,0:T(8,128)S(1)} %copy.25.codes, bf16[16,69,256]{2,1,0:T(8,128)(2,1)S(1)} %bitcast.12, bf16[128,256]{1,0:T(8,128)(2,1)S(1)} %copy-done.4, bf16[256,1024]{1,0:T(8,128)(2,1)S(1)} %copy-done.2, bf16[608,256]{1,0:T(8,128)(2,1)S(1)} %copy-done.3, ...), custom_call_target="tpu_custom_call" | custom-call | tf_op jit(solution)/shard_map/pallas_call | solution.py:415
  109.4 0.8 copy.28
  (3 shorter events, 0.0 us)
Async XLA Ops:
  6.0 5.1 %copy-start.11 = (s32[128,128]{1,0:T(8,128)S(1)}, s32[128,128]{1,0:T(8,128)}, u32[]{:S(2)}) copy-start(s32[128,128]{1,0:T(8,128)} %param.17) | copy-start | bytes 196612
  6.0 5.1 %copy-start.12 = (s32[128,128]{1,0:T(8,128)S(1)}, s32[128,128]{1,0:T(8,128)}, u32[]{:S(2)}) copy-start(s32[128,128]{1,0:T(8,128)} %param.18) | copy-start | bytes 196612
  11.0 7.8 %copy-start.10 = (f32[2,7,7,256]{3,0,2,1:T(2,128)S(1)}, f32[2,7,7,256]{3,0,2,1:T(2,128)}, u32[]{:S(2)}) copy-start(f32[2,7,7,256]{3,0,2,1:T(2,128)} %param.21) | copy-start | bytes 301060
  11.0 7.8 %copy-start.13 = (f32[2,256]{1,0:T(2,128)S(1)}, f32[2,256]{1,0:T(2,128)}, u32[]{:S(2)}) copy-start(f32[2,256]{1,0:T(2,128)} %param.22) | copy-start | bytes 6148
  11.0 7.8 %copy-start = (bf16[2,128,1024]{2,1,0:T(8,128)(2,1)S(1)}, bf16[2,128,1024]{2,1,0:T(8,128)(2,1)}, u32[]{:S(2)}) copy-start(bf16[2,128,1024]{2,1,0:T(8,128)(2,1)} %up_proj.1) | copy-start | bytes 1572868
  11.0 7.8 %copy-start.1 = (bf16[2,1024,128]{2,1,0:T(8,128)(2,1)S(1)}, bf16[2,1024,128]{2,1,0:T(8,128)(2,1)}, u32[]{:S(2)}) copy-start(bf16[2,1024,128]{2,1,0:T(8,128)(2,1)} %down_proj.1) | copy-start | bytes 1572868
  11.0 7.9 %copy-start.2 = (bf16[256,1024]{1,0:T(8,128)(2,1)S(1)}, bf16[256,1024]{1,0:T(8,128)(2,1)}, u32[]{:S(2)}) copy-start(bf16[256,1024]{1,0:T(8,128)(2,1)} %constant.6.clone.pack) | copy-start | bytes 1572868
  11.0 7.9 %copy-start.3 = (bf16[608,256]{1,0:T(8,128)(2,1)S(1)}, bf16[608,256]{1,0:T(8,128)(2,1)}, u32[]{:S(2)}) copy-start(bf16[608,256]{1,0:T(8,128)(2,1)} %constant.7.clone.spread) | copy-start | bytes 933892
  11.0 7.8 %copy-start.4 = (bf16[128,256]{1,0:T(8,128)(2,1)S(1)}, bf16[128,256]{1,0:T(8,128)(2,1)}, u32[]{:S(2)}) copy-start(bf16[128,256]{1,0:T(8,128)(2,1)} %class_table.1) | copy-start | bytes 196612
  11.0 7.8 %copy-start.5 = (f32[2,2048]{1,0:T(2,128)S(1)}, f32[2,2048]{1,0:T(2,128)}, u32[]{:S(2)}) copy-start(f32[2,2048]{1,0:T(2,128)} %up_bias.1) | copy-start | bytes 49156
  11.0 7.8 %copy-start.6 = (f32[2,512]{1,0:T(2,128)S(1)}, f32[2,512]{1,0:T(2,128)}, u32[]{:S(2)}) copy-start(f32[2,512]{1,0:T(2,128)} %norm_gain.1) | copy-start | bytes 12292
  11.0 7.8 %copy-start.7 = (f32[2,512]{1,0:T(2,128)S(1)}, f32[2,512]{1,0:T(2,128)}, u32[]{:S(2)}) copy-start(f32[2,512]{1,0:T(2,128)} %norm_bias.1) | copy-start | bytes 12292
  11.0 7.8 %copy-start.8 = (f32[2,512]{1,0:T(2,128)S(1)}, f32[2,512]{1,0:T(2,128)}, u32[]{:S(2)}) copy-start(f32[2,512]{1,0:T(2,128)} %down_bias.1) | copy-start | bytes 12292
  11.0 7.8 %copy-start.9 = (f32[2,512]{1,0:T(2,128)S(1)}, f32[2,512]{1,0:T(2,128)}, u32[]{:S(2)}) copy-start(f32[2,512]{1,0:T(2,128)} %layer_scale.1) | copy-start | bytes 12292
